TPU v7x, 32 devices: a whole 2x2x4 slice. The times are simulated.
32 devices in a mesh: dp: 2 (over x), section: 4 (over z), space: 4 (over y, core).
Axes of the slice: x: 2, y: 2, z: 4, core: 2. Of those that a mesh axis runs over, the one named last changes fastest.
Arguments:
- images: bfloat16 [4, 4, 64, 256], P('dp', 'space'), may hold values from -6 to 6
- steps: int32 [4], P('dp'), may hold values from 0 to 999
- out_grad: bfloat16 [4, 4, 64, 256], P('dp', 'space'), may hold values from -0.5 to 0.5
- conv_weight: bfloat16 [4, 3, 3, 256, 256], P('section'), may hold values from -0.125 to 0.125
- gn_gain: float32 [4, 256], P('section'), may hold values from 0.5 to 2
- emb_weight: bfloat16 [4, 256, 512], P('section'), may hold values from -0.375 to 0.375
Outputs:
- grad_conv: float32 [4, 3, 3, 256, 256], P('section')
- grad_gain: float32 [4, 256], P('section')
- grad_emb: float32 [4, 256, 512], P('section')
All inputs are finite; a program needn't handle non-finite values.
Results may differ from a plain program's by a relative error of at most 0.0064.
Values may be sent and summed in bfloat16 or wider, within the bound.
A program may use at most 64 MiB of HBM per device.

v0:
```python
import math

import jax
import jax.numpy as jnp
from jax import lax
from jax.sharding import PartitionSpec as P

G = 32
FREQ = 256
MICRO = 2


EPS = 1e-05


def from_behind(value, axis, steps):
    count = lax.axis_size(axis)
    initial, last = (max(0, -steps), min(count, count - steps))
    return lax.ppermute(value, axis, [(source, source + steps) for source in range(initial, last)])


def extended(shard, sides, width):
    for axis, dim in sides:
        size, length = (lax.axis_size(axis), shard.shape[dim])
        up = [(i, (i + 1) % size) for i in range(size - 1)]
        down = [(j, i) for i, j in up]
        last = lax.slice_in_dim(shard, length - width, length, axis=dim)
        initial = lax.slice_in_dim(shard, 0, width, axis=dim)
        before = lax.ppermute(last, axis, up)
        after = lax.ppermute(initial, axis, down)
        shard = jnp.concatenate([before, shard, after], axis=dim)
    return shard


def sinusoid(timesteps, feature_n):
    half_n = feature_n // 2
    freqs = jnp.exp(-math.log(10000.0) * jnp.arange(half_n, dtype=jnp.float32) / half_n)
    angles = timesteps.astype(jnp.float32)[:, None] * freqs[None, :]
    return jnp.concatenate([jnp.cos(angles), jnp.sin(angles)], axis=1)


def group_sums(tensor, groups):
    batch_n, height_n, width_n, channels = tensor.shape
    split = tensor.reshape(batch_n, height_n, width_n, groups, channels // groups)
    return (jnp.sum(split, axis=(1, 2, 4)), jnp.sum(split * split, axis=(1, 2, 4)))


def spread(values, channels):
    return jnp.repeat(values, channels // values.shape[1], axis=1)[:, None, None, :]


def normalize(tensor, first_sum, square_sum, gains, scales, shifts, cell_count):
    channels = tensor.shape[3]
    average = first_sum / cell_count
    inverse = lax.rsqrt(square_sum / cell_count - average * average + EPS)
    normed = (tensor - spread(average, channels)) * spread(inverse, channels) * gains
    return normed * (1.0 + scales[:, None, None, :]) + shifts[:, None, None, :]


def patches(padded, height_n, width_n):
    return jnp.concatenate(
        [
            padded[:, vertical : vertical + height_n, lateral : lateral + width_n, :]
            for vertical in range(3)
            for lateral in range(3)
        ],
        axis=3,
    )


def convolve(padded, matrix):
    batch_n, height_p, width_p, channels = padded.shape
    flat = patches(padded, height_p - 2, width_p - 2).reshape(-1, 9 * channels)
    return jnp.dot(flat, matrix, preferred_element_type=jnp.float32).reshape(
        batch_n, height_p - 2, width_p - 2, matrix.shape[1]
    )


def flip_weight(weight):
    channels = weight.shape[2]
    return jnp.transpose(weight[::-1, ::-1], (0, 1, 3, 2)).reshape(9 * channels, channels)


def silu_slope(pre_act):
    sigmoid_v = jax.nn.sigmoid(pre_act)
    return sigmoid_v * (1.0 + pre_act * (1.0 - sigmoid_v))


def pad_columns(tensor):
    return jnp.pad(tensor, ((0, 0), (0, 0), (1, 1), (0, 0)))


def pick(stacked, index):
    return lax.dynamic_index_in_dim(stacked, index, 0, keepdims=False)


def norm_backward(tensor, first_sum, square_sum, gains, scales, shifts, cell_count, d_pre):

    def mapping(tensor_v, first_v, square_v, gains_v, scales_v, shifts_v):
        return normalize(tensor_v, first_v, square_v, gains_v, scales_v, shifts_v, cell_count)

    _, pull_back = jax.vjp(mapping, tensor, first_sum, square_sum, gains, scales, shifts)
    return pull_back(d_pre)


def per_device(images, steps, out_grad, conv_weight, gn_gain, emb_weight):
    section_count = lax.axis_size("section")
    tick_count = MICRO + section_count - 1
    section_no = lax.axis_index("section")
    local_n = images.shape[0] // MICRO
    row_count = images.shape[1]
    col_count = images.shape[2]
    channels = images.shape[3]
    cell_count = row_count * lax.axis_size("space") * col_count * (channels // G)
    weight = conv_weight[0]
    flat_weight = weight.reshape(9 * channels, channels)
    flipped = flip_weight(weight)
    gains = gn_gain[0]
    all_features = sinusoid(steps, FREQ)
    features = all_features.reshape(MICRO, local_n, FREQ)
    embedded = jnp.dot(
        all_features, emb_weight[0].astype(jnp.float32), precision=lax.Precision.HIGHEST
    ).reshape(MICRO, local_n, 2 * channels)
    batches = images.reshape(MICRO, local_n, row_count, col_count, channels)
    cotangents = out_grad.reshape(MICRO, local_n, row_count, col_count, channels)
    blank = jnp.zeros((local_n, row_count, col_count, channels), jnp.bfloat16)
    carried = blank
    skips = []
    kept_in = []
    kept_first = []
    kept_square = []
    kept_pad = []
    for moment in range(tick_count):
        arrived = blank
        if moment > 0:
            arrived = from_behind(carried, "section", 1)
        inputs = jnp.where(section_no == 0, batches[min(moment, MICRO - 1)], arrived)
        late = moment - (section_count - 1)
        if 0 <= late < MICRO:
            joined = (arrived.astype(jnp.float32) + skips[late].astype(jnp.float32)).astype(
                jnp.bfloat16
            )
            inputs = jnp.where(section_no == section_count - 1, joined, inputs)
        which = jnp.clip(moment - section_no, 0, MICRO - 1)
        chosen = pick(embedded, which)
        tensor = inputs.astype(jnp.float32)
        first_sum, square_sum = group_sums(tensor, G)
        first_sum, square_sum = lax.psum((first_sum, square_sum), "space")
        pre_act = normalize(
            tensor,
            first_sum,
            square_sum,
            gains,
            chosen[:, :channels],
            chosen[:, channels:],
            cell_count,
        )
        activation = jax.nn.silu(pre_act).astype(jnp.bfloat16)
        padded = pad_columns(extended(activation, (("space", 1),), 1))
        conv_out = convolve(padded, flat_weight)
        output = (tensor + conv_out).astype(jnp.bfloat16)
        if moment < MICRO:
            skips.append(from_behind(output, "section", section_count - 1))
        kept_in.append(inputs)
        kept_first.append(first_sum)
        kept_square.append(square_sum)
        kept_pad.append(padded)
        carried = output
    stack_in = jnp.stack(kept_in)
    stack_first = jnp.stack(kept_first)
    stack_square = jnp.stack(kept_square)
    stack_pad = jnp.stack(kept_pad)
    weight_grad = jnp.zeros((9 * channels, channels), jnp.float32)
    gain_grad = jnp.zeros((channels,), jnp.float32)
    emb_grad = jnp.zeros((FREQ, 2 * channels), jnp.float32)
    carried = blank
    skip_grads = []
    for moment in range(tick_count):
        arrived = blank
        if moment > 0:
            arrived = from_behind(carried, "section", -1)
        top_grad = cotangents[moment] if moment < MICRO else blank
        upstream = jnp.where(section_no == section_count - 1, top_grad, arrived)
        early = moment - (section_count - 1)
        if 0 <= early < MICRO:
            joined = (arrived.astype(jnp.float32) + skip_grads[early].astype(jnp.float32)).astype(
                jnp.bfloat16
            )
            upstream = jnp.where(section_no == 0, joined, upstream)
        which_raw = moment - (section_count - 1) + section_no
        valid = (which_raw >= 0) & (which_raw < MICRO)
        upstream = jnp.where(valid, upstream, blank)
        which = jnp.clip(which_raw, 0, MICRO - 1)
        forward_at = jnp.clip(which_raw + section_no, 0, tick_count - 1)
        tensor = pick(stack_in, forward_at).astype(jnp.float32)
        first_sum = pick(stack_first, forward_at)
        square_sum = pick(stack_square, forward_at)
        chosen = pick(embedded, which)
        scales = chosen[:, :channels]
        shifts = chosen[:, channels:]
        pre_act = normalize(tensor, first_sum, square_sum, gains, scales, shifts, cell_count)
        padded = pick(stack_pad, forward_at)
        flat_patch = patches(padded, row_count, col_count).reshape(-1, 9 * channels)
        weight_grad = weight_grad + jnp.dot(
            flat_patch.T, upstream.reshape(-1, channels), preferred_element_type=jnp.float32
        )
        up_pad = pad_columns(extended(upstream, (("space", 1),), 1))
        d_act = convolve(up_pad, flipped)
        d_pre = d_act * silu_slope(pre_act)
        d_tensor, d_first, d_square, d_gains, d_scales, d_shifts = norm_backward(
            tensor, first_sum, square_sum, gains, scales, shifts, cell_count, d_pre
        )
        d_first, d_square = lax.psum((d_first, d_square), "space")
        d_tensor = d_tensor + spread(d_first, channels) + 2.0 * tensor * spread(d_square, channels)
        d_input = (upstream.astype(jnp.float32) + d_tensor).astype(jnp.bfloat16)
        gain_grad = gain_grad + d_gains
        emb_grad = emb_grad + jnp.dot(
            pick(features, which).T,
            jnp.concatenate([d_scales, d_shifts], axis=1),
            precision=lax.Precision.HIGHEST,
        )
        if moment < MICRO:
            skip_grads.append(from_behind(d_input, "section", -(section_count - 1)))
        carried = d_input
    grads = (weight_grad.reshape(1, 3, 3, channels, channels), gain_grad[None], emb_grad[None])
    totals = lax.psum((grads[0], grads[1], grads[2]), ("dp", "space"))
    return (totals[0], totals[1], totals[2])


def solution(mesh):
    in_specs = (
        P("dp", "space", None, None),
        P("dp"),
        P("dp", "space", None, None),
        P("section", None, None, None, None),
        P("section", None),
        P("section", None, None),
    )
    out_specs = (P("section", None, None, None, None), P("section", None), P("section", None, None))
    return jax.shard_map(
        per_device, mesh=mesh, in_specs=in_specs, out_specs=out_specs, check_vma=False
    )
```

profile of v0, /device:TPU:0, one launch (start us, length us, event | category | flops | bytes accessed | tf_op | source)
XLA Modules:
  0.0 289.0 jit_solution(10754524140854845470)
XLA Ops:
  9.3 3.0 %collective-permute-start.16 = (bf16[1,1,64,256]{3,2,1,0:T(8,128)(2,1)S(1)}, bf16[1,1,64,256]{3,2,1,0:T(8,128)(2,1)S(1)}, u32[]{:S(2)}, u32[]{:S(2)}) collective-permute-start(bf16[1,1,64,256]{3,2,1,0:T(8,128)(2,1)S(1)} %select_select_fusion.2), channel_id=1, source_target_pairs={{0,1},{1,2},{2,3},{4,5},{5,6},{6,7},{8,9},{9,10},{10,11},{12,13},{... | collective-permute-start | bytes 98312 | tf_op jit(solution)/shard_map/ppermute | solution.py:29
  14.3 8.3 %all-reduce.19 = (f32[1,32]{1,0:T(1,128)S(1)}, f32[1,32]{1,0:T(1,128)S(1)}) all-reduce(f32[1,32]{1,0:T(1,128)S(1)} %bitcast.533, f32[1,32]{1,0:T(1,128)S(1)} %bitcast.532), channel_id=1, replica_groups=mesh['dp'=2,'section'=4,'space'=4] {'space'}, use_global_device_ids=true, to_apply=%region_5.6 | all-reduce | flops 64 | bytes 512 | tf_op jit(solution)/shard_map/psum | solution.py:148
  26.1 3.0 %collective-permute-start = (bf16[1,1,64,256]{3,2,1,0:T(8,128)(2,1)S(1)}, bf16[1,1,64,256]{3,2,1,0:T(8,128)(2,1)S(1)}, u32[]{:S(2)}, u32[]{:S(2)}) collective-permute-start(bf16[1,1,64,256]{3,2,1,0:T(8,128)(2,1)S(1)} %multiply_convert_fusion.4), channel_id=1, source_target_pairs={{0,1},{1,2},{2,3},{4,5},{5,6},{6,7},{8,9},{9,10},{10,11},{12,13},{... | collective-permute-start | bytes 98312 | tf_op jit(solution)/shard_map/ppermute | solution.py:29
  31.2 1.6 copy.9
  34.8 5.5 %collective-permute-start.9 = (bf16[1,1,64,256]{3,2,1,0:T(8,128)(2,1)S(1)}, bf16[1,1,64,256]{3,2,1,0:T(8,128)(2,1)S(1)}, u32[]{:S(2)}, u32[]{:S(2)}) collective-permute-start(bf16[1,1,64,256]{3,2,1,0:T(8,128)(2,1)S(1)} %fusion.8), channel_id=1, source_target_pairs={{0,12},{1,13},{2,14},{3,15},{16,28},{17,29},{18,30},{19,31}} | collective-permute-start | bytes 98312 | tf_op jit(solution)/shard_map/ppermute | solution.py:19
  48.4 6.5 %all-reduce.18 = (f32[1,32]{1,0:T(1,128)S(1)}, f32[1,32]{1,0:T(1,128)S(1)}) all-reduce(f32[1,32]{1,0:T(1,128)S(1)} %bitcast.534, f32[1,32]{1,0:T(1,128)S(1)} %bitcast.528), channel_id=1, replica_groups=mesh['dp'=2,'section'=4,'space'=4] {'space'}, use_global_device_ids=true, to_apply=%region_11.12 | all-reduce | flops 64 | bytes 512 | tf_op jit(solution)/shard_map/psum | solution.py:148
  56.6 3.0 %collective-permute-start.3 = (bf16[1,1,64,256]{3,2,1,0:T(8,128)(2,1)S(1)}, bf16[1,1,64,256]{3,2,1,0:T(8,128)(2,1)S(1)}, u32[]{:S(2)}, u32[]{:S(2)}) collective-permute-start(bf16[1,1,64,256]{3,2,1,0:T(8,128)(2,1)S(1)} %multiply_convert_fusion.3), channel_id=1, source_target_pairs={{0,1},{1,2},{2,3},{4,5},{5,6},{6,7},{8,9},{9,10},{10,11},{12,13},{... | collective-permute-start | bytes 98312 | tf_op jit(solution)/shard_map/ppermute | solution.py:29
  61.0 1.7 collective-permute-start.13
  66.7 7.1 %all-reduce.17 = (f32[1,32]{1,0:T(1,128)S(1)}, f32[1,32]{1,0:T(1,128)S(1)}) all-reduce(f32[1,32]{1,0:T(1,128)S(1)} %bitcast.535, f32[1,32]{1,0:T(1,128)S(1)} %bitcast.529), channel_id=1, replica_groups=mesh['dp'=2,'section'=4,'space'=4] {'space'}, use_global_device_ids=true, to_apply=%region_17.18 | all-reduce | flops 64 | bytes 512 | tf_op jit(solution)/shard_map/psum | solution.py:148
  75.4 3.0 %collective-permute-start.6 = (bf16[1,1,64,256]{3,2,1,0:T(8,128)(2,1)S(1)}, bf16[1,1,64,256]{3,2,1,0:T(8,128)(2,1)S(1)}, u32[]{:S(2)}, u32[]{:S(2)}) collective-permute-start(bf16[1,1,64,256]{3,2,1,0:T(8,128)(2,1)S(1)} %multiply_convert_fusion.2), channel_id=1, source_target_pairs={{0,1},{1,2},{2,3},{4,5},{5,6},{6,7},{8,9},{9,10},{10,11},{12,13},{... | collective-permute-start | bytes 98312 | tf_op jit(solution)/shard_map/ppermute | solution.py:29
  79.9 4.2 %collective-permute-start.8 = (bf16[1,1,64,256]{3,2,1,0:T(8,128)(2,1)S(1)}, bf16[1,1,64,256]{3,2,1,0:T(8,128)(2,1)S(1)}, u32[]{:S(2)}, u32[]{:S(2)}) collective-permute-start(bf16[1,1,64,256]{3,2,1,0:T(8,128)(2,1)S(1)} %fusion.5), channel_id=1, source_target_pairs={{0,4},{4,8},{8,12},{1,5},{5,9},{9,13},{2,6},{6,10},{10,14},{3,7},{... | collective-permute-start | bytes 98312 | tf_op jit(solution)/shard_map/ppermute | solution.py:19
  86.7 7.8 %all-reduce.16 = (f32[1,32]{1,0:T(1,128)S(1)}, f32[1,32]{1,0:T(1,128)S(1)}) all-reduce(f32[1,32]{1,0:T(1,128)S(1)} %bitcast.536, f32[1,32]{1,0:T(1,128)S(1)} %bitcast.530), channel_id=1, replica_groups=mesh['dp'=2,'section'=4,'space'=4] {'space'}, use_global_device_ids=true, to_apply=%region_23.24 | all-reduce | flops 64 | bytes 512 | tf_op jit(solution)/shard_map/psum | solution.py:148
  96.8 3.0 %collective-permute-start.10 = (bf16[1,1,64,256]{3,2,1,0:T(8,128)(2,1)S(1)}, bf16[1,1,64,256]{3,2,1,0:T(8,128)(2,1)S(1)}, u32[]{:S(2)}, u32[]{:S(2)}) collective-permute-start(bf16[1,1,64,256]{3,2,1,0:T(8,128)(2,1)S(1)} %multiply_convert_fusion.1), channel_id=1, source_target_pairs={{0,1},{1,2},{2,3},{4,5},{5,6},{6,7},{8,9},{9,10},{10,11},{12,13},{... | collective-permute-start | bytes 98312 | tf_op jit(solution)/shard_map/ppermute | solution.py:29
  102.0 4.2 %collective-permute-start.12 = (bf16[1,1,64,256]{3,2,1,0:T(8,128)(2,1)S(1)}, bf16[1,1,64,256]{3,2,1,0:T(8,128)(2,1)S(1)}, u32[]{:S(2)}, u32[]{:S(2)}) collective-permute-start(bf16[1,1,64,256]{3,2,1,0:T(8,128)(2,1)S(1)} %fusion.4), channel_id=1, source_target_pairs={{0,4},{4,8},{8,12},{1,5},{5,9},{9,13},{2,6},{6,10},{10,14},{3,7},{... | collective-permute-start | bytes 98312 | tf_op jit(solution)/shard_map/ppermute | solution.py:19
  108.8 7.8 %all-reduce.15 = (f32[1,32]{1,0:T(1,128)S(1)}, f32[1,32]{1,0:T(1,128)S(1)}) all-reduce(f32[1,32]{1,0:T(1,128)S(1)} %bitcast.537, f32[1,32]{1,0:T(1,128)S(1)} %bitcast.531), channel_id=1, replica_groups=mesh['dp'=2,'section'=4,'space'=4] {'space'}, use_global_device_ids=true, to_apply=%region_29.30 | all-reduce | flops 64 | bytes 512 | tf_op jit(solution)/shard_map/psum | solution.py:148
  120.1 7.2 %all-reduce.14 = (f32[1,32]{1,0:T(1,128)S(1)}, f32[32]{0:T(128)S(1)}) all-reduce(f32[1,32]{1,0:T(1,128)S(1)} %broadcast_multiply_fusion.3, f32[32]{0:T(128)S(1)} %get-tuple-element.68), channel_id=1, replica_groups=mesh['dp'=2,'section'=4,'space'=4] {'space'}, use_global_device_ids=true, to_apply=%region_35.36 | all-reduce | flops 64 | bytes 512 | tf_op jit(solution)/shard_map/psum | solution.py:213
  129.1 4.7 %collective-permute-done.18 = bf16[1,1,64,256]{3,2,1,0:T(8,128)(2,1)S(1)} collective-permute-done((bf16[1,1,64,256]{3,2,1,0:T(8,128)(2,1)S(1)}, bf16[1,1,64,256]{3,2,1,0:T(8,128)(2,1)S(1)}, u32[]{:S(2)}, u32[]{:S(2)}) %collective-permute-start.18) | collective-permute-done | bytes 32800 | tf_op jit(solution)/shard_map/ppermute | solution.py:19
  135.1 3.0 %collective-permute-start.19 = (bf16[1,1,64,256]{3,2,1,0:T(8,128)(2,1)S(1)}, bf16[1,1,64,256]{3,2,1,0:T(8,128)(2,1)S(1)}, u32[]{:S(2)}, u32[]{:S(2)}) collective-permute-start(bf16[1,1,64,256]{3,2,1,0:T(8,128)(2,1)S(1)} %select_select_fusion.1), channel_id=1, source_target_pairs={{0,1},{1,2},{2,3},{4,5},{5,6},{6,7},{8,9},{9,10},{10,11},{12,13},{... | collective-permute-start | bytes 98312 | tf_op jit(solution)/shard_map/ppermute | solution.py:29
  140.9 6.3 %all-reduce.13 = (f32[1,32]{1,0:T(1,128)S(1)}, f32[32]{0:T(128)S(1)}) all-reduce(f32[1,32]{1,0:T(1,128)S(1)} %broadcast_multiply_fusion.2, f32[32]{0:T(128)S(1)} %get-tuple-element.64), channel_id=1, replica_groups=mesh['dp'=2,'section'=4,'space'=4] {'space'}, use_global_device_ids=true, to_apply=%region_41.42 | all-reduce | flops 64 | bytes 512 | tf_op jit(solution)/shard_map/psum | solution.py:213
  148.9 4.5 %collective-permute-done.21 = bf16[1,1,64,256]{3,2,1,0:T(8,128)(2,1)S(1)} collective-permute-done((bf16[1,1,64,256]{3,2,1,0:T(8,128)(2,1)S(1)}, bf16[1,1,64,256]{3,2,1,0:T(8,128)(2,1)S(1)}, u32[]{:S(2)}, u32[]{:S(2)}) %collective-permute-start.21) | collective-permute-done | bytes 32800 | tf_op jit(solution)/shard_map/ppermute | solution.py:19
  154.7 3.0 %collective-permute-start.22 = (bf16[1,1,64,256]{3,2,1,0:T(8,128)(2,1)S(1)}, bf16[1,1,64,256]{3,2,1,0:T(8,128)(2,1)S(1)}, u32[]{:S(2)}, u32[]{:S(2)}) collective-permute-start(bf16[1,1,64,256]{3,2,1,0:T(8,128)(2,1)S(1)} %select_select_fusion), channel_id=1, source_target_pairs={{0,1},{1,2},{2,3},{4,5},{5,6},{6,7},{8,9},{9,10},{10,11},{12,13},{... | collective-permute-start | bytes 98312 | tf_op jit(solution)/shard_map/ppermute | solution.py:29
  162.0 7.2 %all-reduce.12 = (f32[1,32]{1,0:T(1,128)S(1)}, f32[32]{0:T(128)S(1)}) all-reduce(f32[1,32]{1,0:T(1,128)S(1)} %broadcast_multiply_fusion.1, f32[32]{0:T(128)S(1)} %get-tuple-element.60), channel_id=1, replica_groups=mesh['dp'=2,'section'=4,'space'=4] {'space'}, use_global_device_ids=true, to_apply=%region_47.48 | all-reduce | flops 64 | bytes 512 | tf_op jit(solution)/shard_map/psum | solution.py:213
  170.9 4.5 %collective-permute-done.24 = bf16[1,1,64,256]{3,2,1,0:T(8,128)(2,1)S(1)} collective-permute-done((bf16[1,1,64,256]{3,2,1,0:T(8,128)(2,1)S(1)}, bf16[1,1,64,256]{3,2,1,0:T(8,128)(2,1)S(1)}, u32[]{:S(2)}, u32[]{:S(2)}) %collective-permute-start.24) | collective-permute-done | bytes 32800 | tf_op jit(solution)/shard_map/ppermute | solution.py:19
  176.8 3.0 %collective-permute-start.26 = (bf16[1,1,64,256]{3,2,1,0:T(8,128)(2,1)S(1)}, bf16[1,1,64,256]{3,2,1,0:T(8,128)(2,1)S(1)}, u32[]{:S(2)}, u32[]{:S(2)}) collective-permute-start(bf16[1,1,64,256]{3,2,1,0:T(8,128)(2,1)S(1)} %fusion.120), channel_id=1, source_target_pairs={{0,1},{1,2},{2,3},{4,5},{5,6},{6,7},{8,9},{9,10},{10,11},{12,13},{... | collective-permute-start | bytes 98312 | tf_op jit(solution)/shard_map/ppermute | solution.py:29
  181.7 6.9 %all-reduce.11 = (f32[1,32]{1,0:T(1,128)S(1)}, f32[32]{0:T(128)S(1)}) all-reduce(f32[1,32]{1,0:T(1,128)S(1)} %broadcast_multiply_fusion, f32[32]{0:T(128)S(1)} %get-tuple-element.56), channel_id=1, replica_groups=mesh['dp'=2,'section'=4,'space'=4] {'space'}, use_global_device_ids=true, to_apply=%region_53.54 | all-reduce | flops 64 | bytes 512 | tf_op jit(solution)/shard_map/psum | solution.py:213
  190.4 3.0 %collective-permute-start.14 = (bf16[1,1,64,256]{3,2,1,0:T(8,128)(2,1)S(1)}, bf16[1,1,64,256]{3,2,1,0:T(8,128)(2,1)S(1)}, u32[]{:S(2)}, u32[]{:S(2)}) collective-permute-start(bf16[1,1,64,256]{3,2,1,0:T(8,128)(2,1)S(1)} %get-tuple-element.118), channel_id=1, source_target_pairs={{0,1},{1,2},{2,3},{4,5},{5,6},{6,7},{8,9},{9,10},{10,11},{12,13},{... | collective-permute-start | bytes 98312 | tf_op jit(solution)/shard_map/ppermute | solution.py:29
  194.7 4.5 %collective-permute-done.28 = bf16[1,1,64,256]{3,2,1,0:T(8,128)(2,1)S(1)} collective-permute-done((bf16[1,1,64,256]{3,2,1,0:T(8,128)(2,1)S(1)}, bf16[1,1,64,256]{3,2,1,0:T(8,128)(2,1)S(1)}, u32[]{:S(2)}, u32[]{:S(2)}) %collective-permute-start.28) | collective-permute-done | bytes 32800 | tf_op jit(solution)/shard_map/ppermute | solution.py:19
  200.5 3.3 %collective-permute-start.30 = (bf16[1,1,64,256]{3,2,1,0:T(8,128)(2,1)S(1)}, bf16[1,1,64,256]{3,2,1,0:T(8,128)(2,1)S(1)}, u32[]{:S(2)}, u32[]{:S(2)}) collective-permute-start(bf16[1,1,64,256]{3,2,1,0:T(8,128)(2,1)S(1)} %fusion.122), channel_id=1, source_target_pairs={{0,1},{1,2},{2,3},{4,5},{5,6},{6,7},{8,9},{9,10},{10,11},{12,13},{... | collective-permute-start | bytes 98312 | tf_op jit(solution)/shard_map/ppermute | solution.py:29
  206.8 1.9 convolution_add_fusion
  210.5 14.8 %psum.178 = f32[1,256]{1,0:T(1,128)} all-reduce(f32[1,256]{1,0:T(1,128)S(1)} %bitcast.511), channel_id=1, replica_groups=mesh['dp'=2,'section'=4,'space'=4] {'dp','space'}, use_global_device_ids=true, to_apply=%region_60.61 | all-reduce | flops 256 | bytes 2048 | tf_op jit(solution)/shard_map/psum | solution.py:226
  225.3 52.7 %all-reduce.22.cloned.1.call-done = (f32[1,3,3,256,256]{4,3,2,1,0:T(8,128)}, f32[1,256,512]{2,1,0:T(8,128)}) async-done(((f32[1,3,3,256,256]{4,3,2,1,0:T(8,128)}, f32[1,256,512]{2,1,0:T(8,128)}), (f32[1,3,3,256,256]{4,3,2,1,0:T(8,128)}, f32[1,256,512]{2,1,0:T(8,128)})) %all-reduce.22.cloned.1.call-update) | async-done | bytes 2883600 | tf_op jit(solution)/shard_map/psum | solution.py:226
  278.1 3.3 %copy.140 = f32[1,3,3,256,256]{4,3,2,1,0:T(8,128)} copy(f32[1,3,3,256,256]{4,3,2,1,0:T(8,128)} %get-tuple-element.137) | data formatting | bytes 4718592
  (416 shorter events, 68.9 us)
Async XLA Ops:
  7.2 270.9 %all-reduce.22.cloned.1.call-start = ((), (), s32[]{:S(2)}) async-start(), calls=%async_computation | async-start | bytes 5767168 | tf_op jit(solution)/shard_map/psum | solution.py:226
  8.0 33.6 %collective-permute-start.17 = (bf16[1,1,64,256]{3,2,1,0:T(8,128)(2,1)S(1)}, bf16[1,1,64,256]{3,2,1,0:T(8,128)(2,1)S(1)}, u32[]{:S(2)}, u32[]{:S(2)}) collective-permute-start(bf16[1,1,64,256]{3,2,1,0:T(8,128)(2,1)S(1)} %select_select_fusion.2), channel_id=1, source_target_pairs={{1,0},{2,1},{3,2},{5,4},{6,5},{7,6},{9,8},{10,9},{11,10},{13,12},{... | collective-permute-start | bytes 98312 | tf_op jit(solution)/shard_map/ppermute | solution.py:30
  9.3 32.3 %collective-permute-start.16 = (bf16[1,1,64,256]{3,2,1,0:T(8,128)(2,1)S(1)}, bf16[1,1,64,256]{3,2,1,0:T(8,128)(2,1)S(1)}, u32[]{:S(2)}, u32[]{:S(2)}) collective-permute-start(bf16[1,1,64,256]{3,2,1,0:T(8,128)(2,1)S(1)} %select_select_fusion.2), channel_id=1, source_target_pairs={{0,1},{1,2},{2,3},{4,5},{5,6},{6,7},{8,9},{9,10},{10,11},{12,13},{... | collective-permute-start | bytes 98312 | tf_op jit(solution)/shard_map/ppermute | solution.py:29
  24.8 9.0 %collective-permute-start.1 = (bf16[1,1,64,256]{3,2,1,0:T(8,128)(2,1)S(1)}, bf16[1,1,64,256]{3,2,1,0:T(8,128)(2,1)S(1)}, u32[]{:S(2)}, u32[]{:S(2)}) collective-permute-start(bf16[1,1,64,256]{3,2,1,0:T(8,128)(2,1)S(1)} %multiply_convert_fusion.4), channel_id=1, source_target_pairs={{1,0},{2,1},{3,2},{5,4},{6,5},{7,6},{9,8},{10,9},{11,10},{13,12},{... | collective-permute-start | bytes 98312 | tf_op jit(solution)/shard_map/ppermute | solution.py:30
  26.1 7.7 %collective-permute-start = (bf16[1,1,64,256]{3,2,1,0:T(8,128)(2,1)S(1)}, bf16[1,1,64,256]{3,2,1,0:T(8,128)(2,1)S(1)}, u32[]{:S(2)}, u32[]{:S(2)}) collective-permute-start(bf16[1,1,64,256]{3,2,1,0:T(8,128)(2,1)S(1)} %multiply_convert_fusion.4), channel_id=1, source_target_pairs={{0,1},{1,2},{2,3},{4,5},{5,6},{6,7},{8,9},{9,10},{10,11},{12,13},{... | collective-permute-start | bytes 98312 | tf_op jit(solution)/shard_map/ppermute | solution.py:29
  34.8 49.3 %collective-permute-start.9 = (bf16[1,1,64,256]{3,2,1,0:T(8,128)(2,1)S(1)}, bf16[1,1,64,256]{3,2,1,0:T(8,128)(2,1)S(1)}, u32[]{:S(2)}, u32[]{:S(2)}) collective-permute-start(bf16[1,1,64,256]{3,2,1,0:T(8,128)(2,1)S(1)} %fusion.8), channel_id=1, source_target_pairs={{0,12},{1,13},{2,14},{3,15},{16,28},{17,29},{18,30},{19,31}} | collective-permute-start | bytes 98312 | tf_op jit(solution)/shard_map/ppermute | solution.py:19
  40.3 7.0 %collective-permute-start.2 = (bf16[1,1,64,256]{3,2,1,0:T(8,128)(2,1)S(1)}, bf16[1,1,64,256]{3,2,1,0:T(8,128)(2,1)S(1)}, u32[]{:S(2)}, u32[]{:S(2)}) collective-permute-start(bf16[1,1,64,256]{3,2,1,0:T(8,128)(2,1)S(1)} %fusion.8), channel_id=1, source_target_pairs={{0,4},{4,8},{8,12},{1,5},{5,9},{9,13},{2,6},{6,10},{10,14},{3,7},{... | collective-permute-start | bytes 98312 | tf_op jit(solution)/shard_map/ppermute | solution.py:19
  55.3 4.4 %collective-permute-start.4 = (bf16[1,1,64,256]{3,2,1,0:T(8,128)(2,1)S(1)}, bf16[1,1,64,256]{3,2,1,0:T(8,128)(2,1)S(1)}, u32[]{:S(2)}, u32[]{:S(2)}) collective-permute-start(bf16[1,1,64,256]{3,2,1,0:T(8,128)(2,1)S(1)} %multiply_convert_fusion.3), channel_id=1, source_target_pairs={{1,0},{2,1},{3,2},{5,4},{6,5},{7,6},{9,8},{10,9},{11,10},{13,12},{... | collective-permute-start | bytes 98312 | tf_op jit(solution)/shard_map/ppermute | solution.py:30
  56.6 3.9 %collective-permute-start.3 = (bf16[1,1,64,256]{3,2,1,0:T(8,128)(2,1)S(1)}, bf16[1,1,64,256]{3,2,1,0:T(8,128)(2,1)S(1)}, u32[]{:S(2)}, u32[]{:S(2)}) collective-permute-start(bf16[1,1,64,256]{3,2,1,0:T(8,128)(2,1)S(1)} %multiply_convert_fusion.3), channel_id=1, source_target_pairs={{0,1},{1,2},{2,3},{4,5},{5,6},{6,7},{8,9},{9,10},{10,11},{12,13},{... | collective-permute-start | bytes 98312 | tf_op jit(solution)/shard_map/ppermute | solution.py:29
  61.0 45.7 %collective-permute-start.13 = (bf16[1,1,64,256]{3,2,1,0:T(8,128)(2,1)S(1)}, bf16[1,1,64,256]{3,2,1,0:T(8,128)(2,1)S(1)}, u32[]{:S(2)}, u32[]{:S(2)}) collective-permute-start(bf16[1,1,64,256]{3,2,1,0:T(8,128)(2,1)S(1)} %fusion.6), channel_id=1, source_target_pairs={{0,12},{1,13},{2,14},{3,15},{16,28},{17,29},{18,30},{19,31}} | collective-permute-start | bytes 98312 | tf_op jit(solution)/shard_map/ppermute | solution.py:19
  74.1 4.4 %collective-permute-start.7 = (bf16[1,1,64,256]{3,2,1,0:T(8,128)(2,1)S(1)}, bf16[1,1,64,256]{3,2,1,0:T(8,128)(2,1)S(1)}, u32[]{:S(2)}, u32[]{:S(2)}) collective-permute-start(bf16[1,1,64,256]{3,2,1,0:T(8,128)(2,1)S(1)} %multiply_convert_fusion.2), channel_id=1, source_target_pairs={{1,0},{2,1},{3,2},{5,4},{6,5},{7,6},{9,8},{10,9},{11,10},{13,12},{... | collective-permute-start | bytes 98312 | tf_op jit(solution)/shard_map/ppermute | solution.py:30
  75.4 3.9 %collective-permute-start.6 = (bf16[1,1,64,256]{3,2,1,0:T(8,128)(2,1)S(1)}, bf16[1,1,64,256]{3,2,1,0:T(8,128)(2,1)S(1)}, u32[]{:S(2)}, u32[]{:S(2)}) collective-permute-start(bf16[1,1,64,256]{3,2,1,0:T(8,128)(2,1)S(1)} %multiply_convert_fusion.2), channel_id=1, source_target_pairs={{0,1},{1,2},{2,3},{4,5},{5,6},{6,7},{8,9},{9,10},{10,11},{12,13},{... | collective-permute-start | bytes 98312 | tf_op jit(solution)/shard_map/ppermute | solution.py:29
  79.9 5.8 %collective-permute-start.8 = (bf16[1,1,64,256]{3,2,1,0:T(8,128)(2,1)S(1)}, bf16[1,1,64,256]{3,2,1,0:T(8,128)(2,1)S(1)}, u32[]{:S(2)}, u32[]{:S(2)}) collective-permute-start(bf16[1,1,64,256]{3,2,1,0:T(8,128)(2,1)S(1)} %fusion.5), channel_id=1, source_target_pairs={{0,4},{4,8},{8,12},{1,5},{5,9},{9,13},{2,6},{6,10},{10,14},{3,7},{... | collective-permute-start | bytes 98312 | tf_op jit(solution)/shard_map/ppermute | solution.py:19
  95.5 4.4 %collective-permute-start.11 = (bf16[1,1,64,256]{3,2,1,0:T(8,128)(2,1)S(1)}, bf16[1,1,64,256]{3,2,1,0:T(8,128)(2,1)S(1)}, u32[]{:S(2)}, u32[]{:S(2)}) collective-permute-start(bf16[1,1,64,256]{3,2,1,0:T(8,128)(2,1)S(1)} %multiply_convert_fusion.1), channel_id=1, source_target_pairs={{1,0},{2,1},{3,2},{5,4},{6,5},{7,6},{9,8},{10,9},{11,10},{13,12},{... | collective-permute-start | bytes 98312 | tf_op jit(solution)/shard_map/ppermute | solution.py:30
  96.8 3.9 %collective-permute-start.10 = (bf16[1,1,64,256]{3,2,1,0:T(8,128)(2,1)S(1)}, bf16[1,1,64,256]{3,2,1,0:T(8,128)(2,1)S(1)}, u32[]{:S(2)}, u32[]{:S(2)}) collective-permute-start(bf16[1,1,64,256]{3,2,1,0:T(8,128)(2,1)S(1)} %multiply_convert_fusion.1), channel_id=1, source_target_pairs={{0,1},{1,2},{2,3},{4,5},{5,6},{6,7},{8,9},{9,10},{10,11},{12,13},{... | collective-permute-start | bytes 98312 | tf_op jit(solution)/shard_map/ppermute | solution.py:29
  102.0 5.8 %collective-permute-start.12 = (bf16[1,1,64,256]{3,2,1,0:T(8,128)(2,1)S(1)}, bf16[1,1,64,256]{3,2,1,0:T(8,128)(2,1)S(1)}, u32[]{:S(2)}, u32[]{:S(2)}) collective-permute-start(bf16[1,1,64,256]{3,2,1,0:T(8,128)(2,1)S(1)} %fusion.4), channel_id=1, source_target_pairs={{0,4},{4,8},{8,12},{1,5},{5,9},{9,13},{2,6},{6,10},{10,14},{3,7},{... | collective-permute-start | bytes 98312 | tf_op jit(solution)/shard_map/ppermute | solution.py:19
  127.8 6.0 %collective-permute-start.18 = (bf16[1,1,64,256]{3,2,1,0:T(8,128)(2,1)S(1)}, bf16[1,1,64,256]{3,2,1,0:T(8,128)(2,1)S(1)}, u32[]{:S(2)}, u32[]{:S(2)}) collective-permute-start(bf16[1,1,64,256]{3,2,1,0:T(8,128)(2,1)S(1)} %fusion.123), channel_id=1, source_target_pairs={{4,0},{8,4},{12,8},{5,1},{9,5},{13,9},{6,2},{10,6},{14,10},{7,3},{... | collective-permute-start | bytes 98312 | tf_op jit(solution)/shard_map/ppermute | solution.py:19
  133.8 6.0 %collective-permute-start.20 = (bf16[1,1,64,256]{3,2,1,0:T(8,128)(2,1)S(1)}, bf16[1,1,64,256]{3,2,1,0:T(8,128)(2,1)S(1)}, u32[]{:S(2)}, u32[]{:S(2)}) collective-permute-start(bf16[1,1,64,256]{3,2,1,0:T(8,128)(2,1)S(1)} %select_select_fusion.1), channel_id=1, source_target_pairs={{1,0},{2,1},{3,2},{5,4},{6,5},{7,6},{9,8},{10,9},{11,10},{13,12},{... | collective-permute-start | bytes 98312 | tf_op jit(solution)/shard_map/ppermute | solution.py:30
  135.1 4.7 %collective-permute-start.19 = (bf16[1,1,64,256]{3,2,1,0:T(8,128)(2,1)S(1)}, bf16[1,1,64,256]{3,2,1,0:T(8,128)(2,1)S(1)}, u32[]{:S(2)}, u32[]{:S(2)}) collective-permute-start(bf16[1,1,64,256]{3,2,1,0:T(8,128)(2,1)S(1)} %select_select_fusion.1), channel_id=1, source_target_pairs={{0,1},{1,2},{2,3},{4,5},{5,6},{6,7},{8,9},{9,10},{10,11},{12,13},{... | collective-permute-start | bytes 98312 | tf_op jit(solution)/shard_map/ppermute | solution.py:29
  138.2 32.8 %collective-permute-start.25 = (bf16[1,1,64,256]{3,2,1,0:T(8,128)(2,1)S(1)}, bf16[1,1,64,256]{3,2,1,0:T(8,128)(2,1)S(1)}, u32[]{:S(2)}, u32[]{:S(2)}) collective-permute-start(bf16[1,1,64,256]{3,2,1,0:T(8,128)(2,1)S(1)} %fusion.123), channel_id=1, source_target_pairs={{12,0},{13,1},{14,2},{15,3},{28,16},{29,17},{30,18},{31,19}} | collective-permute-start | bytes 98312 | tf_op jit(solution)/shard_map/ppermute | solution.py:19
  147.6 5.8 %collective-permute-start.21 = (bf16[1,1,64,256]{3,2,1,0:T(8,128)(2,1)S(1)}, bf16[1,1,64,256]{3,2,1,0:T(8,128)(2,1)S(1)}, u32[]{:S(2)}, u32[]{:S(2)}) collective-permute-start(bf16[1,1,64,256]{3,2,1,0:T(8,128)(2,1)S(1)} %fusion.75), channel_id=1, source_target_pairs={{4,0},{8,4},{12,8},{5,1},{9,5},{13,9},{6,2},{10,6},{14,10},{7,3},{... | collective-permute-start | bytes 98312 | tf_op jit(solution)/shard_map/ppermute | solution.py:19
  153.4 7.6 %collective-permute-start.23 = (bf16[1,1,64,256]{3,2,1,0:T(8,128)(2,1)S(1)}, bf16[1,1,64,256]{3,2,1,0:T(8,128)(2,1)S(1)}, u32[]{:S(2)}, u32[]{:S(2)}) collective-permute-start(bf16[1,1,64,256]{3,2,1,0:T(8,128)(2,1)S(1)} %select_select_fusion), channel_id=1, source_target_pairs={{1,0},{2,1},{3,2},{5,4},{6,5},{7,6},{9,8},{10,9},{11,10},{13,12},{... | collective-permute-start | bytes 98312 | tf_op jit(solution)/shard_map/ppermute | solution.py:30
  154.7 6.3 %collective-permute-start.22 = (bf16[1,1,64,256]{3,2,1,0:T(8,128)(2,1)S(1)}, bf16[1,1,64,256]{3,2,1,0:T(8,128)(2,1)S(1)}, u32[]{:S(2)}, u32[]{:S(2)}) collective-permute-start(bf16[1,1,64,256]{3,2,1,0:T(8,128)(2,1)S(1)} %select_select_fusion), channel_id=1, source_target_pairs={{0,1},{1,2},{2,3},{4,5},{5,6},{6,7},{8,9},{9,10},{10,11},{12,13},{... | collective-permute-start | bytes 98312 | tf_op jit(solution)/shard_map/ppermute | solution.py:29
  159.7 35.1 %collective-permute-start.29 = (bf16[1,1,64,256]{3,2,1,0:T(8,128)(2,1)S(1)}, bf16[1,1,64,256]{3,2,1,0:T(8,128)(2,1)S(1)}, u32[]{:S(2)}, u32[]{:S(2)}) collective-permute-start(bf16[1,1,64,256]{3,2,1,0:T(8,128)(2,1)S(1)} %fusion.75), channel_id=1, source_target_pairs={{12,0},{13,1},{14,2},{15,3},{28,16},{29,17},{30,18},{31,19}} | collective-permute-start | bytes 98312 | tf_op jit(solution)/shard_map/ppermute | solution.py:19
  169.6 5.8 %collective-permute-start.24 = (bf16[1,1,64,256]{3,2,1,0:T(8,128)(2,1)S(1)}, bf16[1,1,64,256]{3,2,1,0:T(8,128)(2,1)S(1)}, u32[]{:S(2)}, u32[]{:S(2)}) collective-permute-start(bf16[1,1,64,256]{3,2,1,0:T(8,128)(2,1)S(1)} %fusion.79), channel_id=1, source_target_pairs={{4,0},{8,4},{12,8},{5,1},{9,5},{13,9},{6,2},{10,6},{14,10},{7,3},{... | collective-permute-start | bytes 98312 | tf_op jit(solution)/shard_map/ppermute | solution.py:19
  175.5 4.4 %collective-permute-start.27 = (bf16[1,1,64,256]{3,2,1,0:T(8,128)(2,1)S(1)}, bf16[1,1,64,256]{3,2,1,0:T(8,128)(2,1)S(1)}, u32[]{:S(2)}, u32[]{:S(2)}) collective-permute-start(bf16[1,1,64,256]{3,2,1,0:T(8,128)(2,1)S(1)} %fusion.120), channel_id=1, source_target_pairs={{1,0},{2,1},{3,2},{5,4},{6,5},{7,6},{9,8},{10,9},{11,10},{13,12},{... | collective-permute-start | bytes 98312 | tf_op jit(solution)/shard_map/ppermute | solution.py:30
  176.8 3.9 %collective-permute-start.26 = (bf16[1,1,64,256]{3,2,1,0:T(8,128)(2,1)S(1)}, bf16[1,1,64,256]{3,2,1,0:T(8,128)(2,1)S(1)}, u32[]{:S(2)}, u32[]{:S(2)}) collective-permute-start(bf16[1,1,64,256]{3,2,1,0:T(8,128)(2,1)S(1)} %fusion.120), channel_id=1, source_target_pairs={{0,1},{1,2},{2,3},{4,5},{5,6},{6,7},{8,9},{9,10},{10,11},{12,13},{... | collective-permute-start | bytes 98312 | tf_op jit(solution)/shard_map/ppermute | solution.py:29
  189.1 14.8 %collective-permute-start.15 = (bf16[1,1,64,256]{3,2,1,0:T(8,128)(2,1)S(1)}, bf16[1,1,64,256]{3,2,1,0:T(8,128)(2,1)S(1)}, u32[]{:S(2)}, u32[]{:S(2)}) collective-permute-start(bf16[1,1,64,256]{3,2,1,0:T(8,128)(2,1)S(1)} %get-tuple-element.118), channel_id=1, source_target_pairs={{1,0},{2,1},{3,2},{5,4},{6,5},{7,6},{9,8},{10,9},{11,10},{13,12},{... | collective-permute-start | bytes 98312 | tf_op jit(solution)/shard_map/ppermute | solution.py:30
  190.4 13.5 %collective-permute-start.14 = (bf16[1,1,64,256]{3,2,1,0:T(8,128)(2,1)S(1)}, bf16[1,1,64,256]{3,2,1,0:T(8,128)(2,1)S(1)}, u32[]{:S(2)}, u32[]{:S(2)}) collective-permute-start(bf16[1,1,64,256]{3,2,1,0:T(8,128)(2,1)S(1)} %get-tuple-element.118), channel_id=1, source_target_pairs={{0,1},{1,2},{2,3},{4,5},{5,6},{6,7},{8,9},{9,10},{10,11},{12,13},{... | collective-permute-start | bytes 98312 | tf_op jit(solution)/shard_map/ppermute | solution.py:29
  193.4 5.8 %collective-permute-start.28 = (bf16[1,1,64,256]{3,2,1,0:T(8,128)(2,1)S(1)}, bf16[1,1,64,256]{3,2,1,0:T(8,128)(2,1)S(1)}, u32[]{:S(2)}, u32[]{:S(2)}) collective-permute-start(bf16[1,1,64,256]{3,2,1,0:T(8,128)(2,1)S(1)} %get-tuple-element.117), channel_id=1, source_target_pairs={{4,0},{8,4},{12,8},{5,1},{9,5},{13,9},{6,2},{10,6},{14,10},{7,3},{... | collective-permute-start | bytes 98312 | tf_op jit(solution)/shard_map/ppermute | solution.py:19
  199.2 9.5 %collective-permute-start.31 = (bf16[1,1,64,256]{3,2,1,0:T(8,128)(2,1)S(1)}, bf16[1,1,64,256]{3,2,1,0:T(8,128)(2,1)S(1)}, u32[]{:S(2)}, u32[]{:S(2)}) collective-permute-start(bf16[1,1,64,256]{3,2,1,0:T(8,128)(2,1)S(1)} %fusion.122), channel_id=1, source_target_pairs={{1,0},{2,1},{3,2},{5,4},{6,5},{7,6},{9,8},{10,9},{11,10},{13,12},{... | collective-permute-start | bytes 98312 | tf_op jit(solution)/shard_map/ppermute | solution.py:30
  200.5 8.3 %collective-permute-start.30 = (bf16[1,1,64,256]{3,2,1,0:T(8,128)(2,1)S(1)}, bf16[1,1,64,256]{3,2,1,0:T(8,128)(2,1)S(1)}, u32[]{:S(2)}, u32[]{:S(2)}) collective-permute-start(bf16[1,1,64,256]{3,2,1,0:T(8,128)(2,1)S(1)} %fusion.122), channel_id=1, source_target_pairs={{0,1},{1,2},{2,3},{4,5},{5,6},{6,7},{8,9},{9,10},{10,11},{12,13},{... | collective-permute-start | bytes 98312 | tf_op jit(solution)/shard_map/ppermute | solution.py:29
  (29 other events, 261.3 us)
Sparse Core Ops, SparseCore 0:
  210.6 67.4 all-reduce.21
where the time goes:
time: 290 us; the launch traced here: 289 us
  blocking collectives  79.9 us (28%)
  waiting for transfers between devices  78.3 us (27%)
  starting transfers between devices  69.5 us (24%)
  local copies, waits for them, and re-layouts  20.9 us (7%)
  between operations  16.3 us (6%)
  other arithmetic  15.7 us (5%)
  matrix products  8.32 us (3%)
    psum x1, waiting for transfers between devices, per_device(): totals = lax.psum((grads[0], grads[1], grads[2]), ('dp', 'space'))  52.7 us
    psum x5, blocking collectives, per_device(): first_sum, square_sum = lax.psum((first_sum, square_sum), 'space')  37.4 us
    ppermute x10, starting transfers between devices, extended(): before = lax.ppermute(last, axis, up)  30.6 us
    psum x4, blocking collectives, per_device(): d_first, d_square = lax.psum((d_first, d_square), 'space')  27.7 us
    ppermute x12, starting transfers between devices, from_behind(): lax.ppermute(value, axis, [(source, source + steps) for source in range(i...  26 us
    ppermute x12, waiting for transfers between devices, from_behind(): lax.ppermute(value, axis, [(source, source + steps) for source in range(i...  22.3 us
    psum x1, blocking collectives, per_device(): totals = lax.psum((grads[0], grads[1], grads[2]), ('dp', 'space'))  14.8 us
    ppermute x10, starting transfers between devices, extended(): after = lax.ppermute(initial, axis, down)  12.9 us
  transfers between devices with their start and end apart: 33, of which 12 were waited for; matrix products, arithmetic and copies ran while one was open for 11% of the time, Pallas kernels for 0%

commit v1 on v0

v1 whole, which is shorter than its diff:
```python
import functools
import math

import jax
import jax.numpy as jnp
import numpy as np
from jax import lax
from jax.experimental import pallas as pl
from jax.experimental.pallas import tpu as pltpu
from jax.sharding import PartitionSpec as P

G = 32
EPS = 1e-05
MESH = pl.DeviceIdType.MESH
F32 = jnp.float32
BF16 = jnp.bfloat16
PIX = 256
COLS = 64
C = 256


def thirds(x):
    first = x.astype(BF16)
    rest = x - first.astype(F32)
    second = rest.astype(BF16)
    return first, second, (rest - second.astype(F32)).astype(BF16)


def exact_dot(x, matrix):
    parts = [jnp.dot(part, matrix, preferred_element_type=F32) for part in thirds(x)]
    return parts[0] + (parts[1] + parts[2])


def rows_of(*rows):
    index = lax.broadcasted_iota(jnp.int32, (8, rows[0].shape[1]), 0)
    out = jnp.zeros((8, rows[0].shape[1]), F32)
    for i, row in enumerate(rows):
        out = jnp.where(index == i, row, out)
    return out


def spread_columns(ref, value):
    column = lax.broadcasted_iota(jnp.int32, (PIX, C), 0) & (COLS - 1)
    left = jnp.where(column == 0, 0.0, pltpu.roll(value, 1, 0))
    right = jnp.where(column == COLS - 1, 0.0, pltpu.roll(value, PIX - 1, 0))
    ref[COLS : COLS + PIX, 0:C] = left.astype(BF16)
    ref[COLS : COLS + PIX, C : 2 * C] = value.astype(BF16)
    ref[COLS : COLS + PIX, 2 * C : 3 * C] = right.astype(BF16)


def clear_border(ref):
    blank = jnp.zeros((COLS, 3 * C), BF16)
    ref[0:COLS, :] = blank
    ref[COLS + PIX : 2 * COLS + PIX, :] = blank


def convolve(ref, kernel_of):
    total = None
    for ky in range(3):
        part = jnp.dot(
            ref[ky * COLS : ky * COLS + PIX, :], kernel_of(ky), preferred_element_type=F32
        )
        total = part if total is None else total + part
    return total


def body(
    n_sec, flips, steps, freqs, images, out_grad, weight, gain, emb,
    conv_out, gain_out, emb_out,
    hbuf, skip, gskip, obuf, dbuf, act_t, g_all, small, turned, act_cols, g_cols,
    normed, slope, d_act, send, recv,
):
    dp = lax.axis_index("dp")
    s = lax.axis_index("section")
    space = lax.axis_index("space")
    y = space // 2
    last = n_sec - 1
    part = lax.rem(dp, 2)
    me = part * 2 + y
    ahead, behind = lax.rem(s + 1, n_sec), lax.rem(s + n_sec - 1, n_sec)

    def space_peer(k):
        return {"space": space ^ k}

    def plane_peer(k):
        if k == 2:
            return {"space": space ^ 2}
        return {"dp": dp ^ 1, "space": space ^ (k & 2)}

    barrier = pltpu.get_barrier_semaphore()
    partners = [space_peer(k) for k in (1, 2, 3)]
    partners += [plane_peer(k) for k in flips if k != 2]
    partners += [{"section": ahead}, {"section": behind}]
    for partner in partners:
        pl.semaphore_signal(barrier, inc=1, device_id=partner, device_id_type=MESH)

    def remote(src, dst, number, device):
        return pltpu.make_async_remote_copy(
            src_ref=src, dst_ref=dst, send_sem=send.at[number], recv_sem=recv.at[number],
            device_id=device, device_id_type=MESH,
        )

    def row_at(index):
        return pl.ds(pl.multiple_of(index * COLS, COLS), COLS)

    g_mine = g_all.at[me]
    g_cols_mine = g_cols.at[me]

    def image_row(k):
        return remote(
            images.at[(space ^ k) // 2, 0], hbuf.at[row_at(space), :], k - 1, space_peer(k)
        )

    def grad_row(k):
        return remote(
            out_grad.at[(space ^ k) // 2, 0], g_all.at[me ^ (k >> 1), row_at(space), :],
            k - 1, space_peer(k),
        )

    forward_hop = remote(obuf, hbuf, 3, {"section": ahead})
    forward_skip = remote(obuf, skip, 4, {"section": behind})
    backward_hop = remote(dbuf, g_mine, 5, {"section": behind})
    backward_skip = remote(dbuf, gskip, 6, {"section": ahead})
    act_copy = {k: remote(act_t.at[me], act_t.at[me], 6 + k, plane_peer(k)) for k in flips}
    g_copy = {k: remote(g_mine, g_mine, 9 + k, plane_peer(k)) for k in flips}
    small_copy = {k: remote(small.at[me], small.at[me], 12 + k, plane_peer(k)) for k in flips}

    angles = steps[y].astype(F32) * freqs[...]
    features = jnp.concatenate([jnp.cos(angles), jnp.sin(angles)], axis=1)
    embedded = exact_dot(jnp.broadcast_to(features, (8, C)), emb[0])[0:1]
    scales1 = 1.0 + embedded[:, :C]
    shifts = embedded[:, C:]
    gains = gain[...]
    factor = gains * scales1
    same = (
        lax.broadcasted_iota(jnp.int32, (C, C), 0) // (C // G)
        == lax.broadcasted_iota(jnp.int32, (C, C), 1) // (C // G)
    ).astype(F32).astype(BF16)
    cells = PIX * (C // G)

    clear_border(act_cols)
    for i in range(4):
        clear_border(g_cols.at[i])

    pl.semaphore_wait(barrier, len(partners))

    def turn_weights():
        for ky in range(3):
            for kx in range(3):
                turned[ky, kx * C : (kx + 1) * C, :] = weight[0, 2 - ky, 2 - kx].T

    def back_convolve():
        spread_columns(g_cols_mine, g_mine[...].astype(F32))
        d_act[...] = convolve(g_cols_mine, lambda ky: turned[ky])

    def share_grad():
        for k in flips:
            g_copy[k].start()

    @pl.when(s == 0)
    def _():
        for k in (1, 2, 3):
            image_row(k).start()
        hbuf[row_at(space), :] = images[y, 0]
        for k in (1, 2, 3):
            image_row(k).wait_recv()

    @pl.when(s == last)
    def _():
        for k in (1, 2, 3):
            grad_row(k).start()
        g_all[me, row_at(space), :] = out_grad[y, 0]
        turn_weights()
        for k in (1, 2, 3):
            grad_row(k).wait_recv()
        share_grad()
        back_convolve()

    @pl.when(s > 0)
    def _():
        forward_hop.wait_recv()

    @pl.when(s == last)
    def _():
        forward_skip.wait_recv()
        hbuf[...] = (hbuf[...].astype(F32) + skip[...].astype(F32)).astype(BF16)

    tensor = hbuf[...].astype(F32)
    first = jnp.sum(tensor, axis=0, keepdims=True)
    square = jnp.sum(tensor * tensor, axis=0, keepdims=True)
    sums = exact_dot(rows_of(first, square), same) * (1.0 / cells)
    average = sums[0:1]
    inverse = lax.rsqrt(sums[1:2] - average * average + EPS)
    normal = (tensor - average) * inverse
    normed[...] = normal
    pre = normal * factor + shifts
    sigmoid = jax.nn.sigmoid(pre)
    act = pre * sigmoid

    @pl.when(s < last)
    def _():
        spread_columns(act_cols, act)
        out = convolve(act_cols, lambda ky: weight[0, ky].reshape(3 * C, C))
        obuf[...] = (hbuf[...].astype(F32) + out).astype(BF16)
        forward_hop.start()

    @pl.when(s == 0)
    def _():
        forward_skip.start()

    slope[...] = sigmoid * (1.0 + pre * (1.0 - sigmoid))
    act_t[me] = act.astype(BF16).T
    for k in flips:
        act_copy[k].start()

    @pl.when(s < last)
    def _():
        turn_weights()
        backward_hop.wait_recv()

    @pl.when(s == 0)
    def _():
        backward_skip.wait_recv()
        g_all[me] = (g_mine[...].astype(F32) + gskip[...].astype(F32)).astype(BF16)

    @pl.when(s < last)
    def _():
        share_grad()
        back_convolve()

    d_pre = d_act[...] * slope[...]
    normal = normed[...]
    sum_pre = jnp.sum(d_pre, axis=0, keepdims=True)
    sum_normal = jnp.sum(d_pre * normal, axis=0, keepdims=True)

    @pl.when(s > 0)
    def _():
        means = exact_dot(rows_of(sum_pre * factor, sum_normal * factor), same) * (1.0 / cells)
        d_tensor = inverse * (d_pre * factor - means[0:1] - normal * means[1:2])
        dbuf[...] = (g_mine[...].astype(F32) + d_tensor).astype(BF16)
        backward_hop.start()

    @pl.when(s == last)
    def _():
        backward_skip.start()

    small[me] = rows_of(sum_normal * gains, sum_pre, sum_normal * scales1, features)
    for k in flips:
        small_copy[k].start()

    for k in flips:
        act_copy[k].wait_recv()
    for k in flips:
        g_copy[k].wait_recv()
        other = me ^ (((k & 1) << 1) | (k >> 1))
        spread_columns(g_cols.at[other], g_all[other].astype(F32))
    if len(flips) == 3:
        slots = [0, 1, 2, 3]
    else:
        slots = [part * 2, part * 2 + 1]
    for ky in range(3):
        for kx in range(3):
            total = None
            for i in slots:
                piece = jnp.dot(
                    act_t[i],
                    g_cols[i, ky * COLS : ky * COLS + PIX, kx * C : (kx + 1) * C],
                    preferred_element_type=F32,
                )
                total = piece if total is None else total + piece
            conv_out[0, 2 - ky, 2 - kx] = total

    for k in flips:
        small_copy[k].wait_recv()
    packed = [small[i] for i in slots]
    gain_total = packed[0][2:3]
    for block in packed[1:]:
        gain_total = gain_total + block[2:3]
    gain_out[...] = gain_total
    feature_rows = rows_of(*[block[3:4] for block in packed])
    d_rows = rows_of(*[jnp.concatenate([block[0:1], block[1:2]], axis=1) for block in packed])
    emb_out[0] = jnp.dot(
        feature_rows.T, d_rows, precision=lax.Precision.HIGHEST, preferred_element_type=F32
    )

    @pl.when(s == 0)
    def _():
        for k in (1, 2, 3):
            image_row(k).wait_send()
        forward_skip.wait_send()

    @pl.when(s == last)
    def _():
        for k in (1, 2, 3):
            grad_row(k).wait_send()
        backward_skip.wait_send()

    @pl.when(s < last)
    def _():
        forward_hop.wait_send()

    @pl.when(s > 0)
    def _():
        backward_hop.wait_send()

    for k in flips:
        act_copy[k].wait_send()
        g_copy[k].wait_send()
        small_copy[k].wait_send()


def per_device(images, steps, out_grad, conv_weight, gn_gain, emb_weight):
    n_dp = lax.axis_size("dp")
    n_sec = lax.axis_size("section")
    flips = (1, 2, 3) if n_dp == 2 else (2,)
    half = C // 2
    freqs = np.exp(-math.log(10000.0) * np.arange(half, dtype=np.float32) / half)
    vmem = pl.BlockSpec(memory_space=pltpu.VMEM)
    grads = pl.pallas_call(
        functools.partial(body, n_sec, flips),
        out_shape=(
            jax.ShapeDtypeStruct((1, 3, 3, C, C), F32),
            jax.ShapeDtypeStruct((1, C), F32),
            jax.ShapeDtypeStruct((1, C, 2 * C), F32),
        ),
        in_specs=[pl.BlockSpec(memory_space=pltpu.SMEM)] + [vmem] * 6,
        out_specs=(vmem, vmem, vmem),
        scratch_shapes=[
            pltpu.VMEM((PIX, C), BF16),
            pltpu.VMEM((PIX, C), BF16),
            pltpu.VMEM((PIX, C), BF16),
            pltpu.VMEM((PIX, C), BF16),
            pltpu.VMEM((PIX, C), BF16),
            pltpu.VMEM((4, C, PIX), BF16),
            pltpu.VMEM((4, PIX, C), BF16),
            pltpu.VMEM((4, 8, C), F32),
            pltpu.VMEM((3, 3 * C, C), BF16),
            pltpu.VMEM((PIX + 2 * COLS, 3 * C), BF16),
            pltpu.VMEM((4, PIX + 2 * COLS, 3 * C), BF16),
            pltpu.VMEM((PIX, C), F32),
            pltpu.VMEM((PIX, C), F32),
            pltpu.VMEM((PIX, C), F32),
            pltpu.SemaphoreType.DMA((16,)),
            pltpu.SemaphoreType.DMA((16,)),
        ],
        compiler_params=pltpu.CompilerParams(
            collective_id=0, has_side_effects=True, vmem_limit_bytes=40 * 1024 * 1024
        ),
    )(
        steps, jnp.asarray(freqs, F32)[None, :], images, out_grad, conv_weight, gn_gain, emb_weight
    )
    if n_dp != 2:
        grads = lax.psum(grads, "dp")
    return grads


def solution(mesh):
    in_specs = (
        P("dp", "space", None, None),
        P("dp"),
        P("dp", "space", None, None),
        P("section", None, None, None, None),
        P("section", None),
        P("section", None, None),
    )
    out_specs = (P("section", None, None, None, None), P("section", None), P("section", None, None))
    return jax.shard_map(
        per_device, mesh=mesh, in_specs=in_specs, out_specs=out_specs, check_vma=False
    )
```

time: 290 us -> 58.8 us (0.20)
  blocking collectives: 79.9 us -> 0 us
  waiting for transfers between devices: 78.3 us -> 0 us
  starting transfers between devices: 69.5 us -> 0 us
  Pallas kernels: 0 us -> 49.2 us
  other arithmetic: 15.7 us -> 0 us
  between operations: 16.3 us -> 0.66 us
  local copies, waits for them, and re-layouts: 20.9 us -> 8.64 us
  matrix products: 8.32 us -> 0 us
    psum x10 -> x0, blocking collectives: 79.9 us -> none  [the longest x5 37.4 us: per_device(): first_sum, square_sum = lax.psum((first_sum, square_sum), 'space')]
    ppermute x32 -> x0, starting transfers between devices: 69.5 us -> none  [the longest x10 30.6 us: extended(): before = lax.ppermute(last, axis, up)]
    psum x1 -> x0, waiting for transfers between devices: 52.7 us -> none  [per_device(): totals = lax.psum((grads[0], grads[1], grads[2]), ('dp', 'space'))]
    pallas_call x0 -> x1, Pallas kernels: none -> 49.2 us  [per_device(): pl.pallas_call(functools.partial(body, n_sec, flips), out_shape=(jax.Shap...]
    ppermute x32 -> x0, waiting for transfers between devices: 25.6 us -> none  [the longest x12 22.3 us: from_behind(): lax.ppermute(value, axis, [(source, source + steps) for source in range(i...]
    dot_general x15 -> x0, matrix products: 8.32 us -> none  [the longest x9 4.2 us: convolve(): jnp.dot(flat, matrix, preferred_element_type=jnp.float32)]
    unnamed x14 -> x0, other arithmetic: 4.92 us -> none
    broadcast_in_dim x56 -> x0, local copies, waits for them, and re-layouts: 4.49 us -> none  [spread(): jnp.repeat(values, channels // values.shape[1], axis=1)[:, None, None, :]]
  transfers between devices with their start and end apart: 33 -> 0, of which waited for: 12 -> 0; matrix products, arithmetic and copies ran while one was open for 11% -> 0% of each run, Pallas kernels for 0% -> 0%
where the time goes in v1:
time: 58.8 us; the launch traced here: 58.5 us
  Pallas kernels  49.2 us (84%)
  local copies, waits for them, and re-layouts  8.64 us (15%)
  between operations  0.66 us (1%)
    pallas_call x1, Pallas kernels, per_device(): pl.pallas_call(functools.partial(body, n_sec, flips), out_shape=(jax.Shap...  49.2 us
    unnamed x17, local copies, waits for them, and re-layouts  8.64 us

profile of v1, /device:TPU:0, one launch (start us, length us, event | category | flops | bytes accessed | tf_op | source)
XLA Modules:
  0.0 58.5 jit_solution(3347806458065491778)
XLA Ops:
  0.6 0.0 copy-start
  0.6 1.3 %copy-done = bf16[1,3,3,256,256]{4,3,2,1,0:T(8,128)(2,1)S(1)} copy-done((bf16[1,3,3,256,256]{4,3,2,1,0:T(8,128)(2,1)S(1)}, bf16[1,3,3,256,256]{4,3,2,1,0:T(8,128)(2,1)}, u32[]{:S(2)}) %copy-start) | copy-done | bytes 1179672
  1.9 0.0 copy-start.1
  1.9 0.9 %copy-done.1 = bf16[1,256,512]{2,1,0:T(8,128)(2,1)S(1)} copy-done((bf16[1,256,512]{2,1,0:T(8,128)(2,1)S(1)}, bf16[1,256,512]{2,1,0:T(8,128)(2,1)}, u32[]{:S(2)}) %copy-start.1) | copy-done | bytes 262168
  2.9 0.0 copy-start.2
  2.9 0.8 %copy-done.2 = bf16[2,1,64,256]{3,2,1,0:T(8,128)(2,1)S(1)} copy-done((bf16[2,1,64,256]{3,2,1,0:T(8,128)(2,1)S(1)}, bf16[2,1,64,256]{3,2,1,0:T(8,128)(2,1)}, u32[]{:S(2)}) %copy-start.2) | copy-done | bytes 65560
  3.7 0.0 copy-start.3
  3.7 0.8 %copy-done.3 = bf16[2,1,64,256]{3,2,1,0:T(8,128)(2,1)S(1)} copy-done((bf16[2,1,64,256]{3,2,1,0:T(8,128)(2,1)S(1)}, bf16[2,1,64,256]{3,2,1,0:T(8,128)(2,1)}, u32[]{:S(2)}) %copy-start.3) | copy-done | bytes 65560
  4.5 0.0 copy-start.4
  4.5 0.7 %copy-done.4 = f32[1,256]{1,0:T(1,128)S(1)} copy-done((f32[1,256]{1,0:T(1,128)S(1)}, f32[1,256]{1,0:T(1,128)}, u32[]{:S(2)}) %copy-start.4) | copy-done | bytes 1048
  5.2 0.0 copy-start.5
  5.2 0.7 %copy-done.5 = s32[2]{0:T(128)S(1)} copy-done((s32[2]{0:T(128)S(1)}, s32[2]{0:T(128)}, u32[]{:S(2)}) %copy-start.5) | copy-done | bytes 32
  5.9 0.0 copy-start.6
  5.9 0.7 %copy-done.6 = f32[1,128]{1,0:T(1,128)S(1)} copy-done((f32[1,128]{1,0:T(1,128)S(1)}, f32[1,128]{1,0:T(1,128)}, u32[]{:S(2)}) %copy-start.6) | copy-done | bytes 536
  6.5 49.2 %shard_map.94 = (f32[1,3,3,256,256]{4,3,2,1,0:T(8,128)S(1)}, f32[1,256]{1,0:T(1,128)S(1)}, f32[1,256,512]{2,1,0:T(8,128)S(1)}) custom-call(s32[2]{0:T(128)S(1)} %copy-done.5, f32[1,128]{1,0:T(1,128)S(1)} %copy-done.6, bf16[2,1,64,256]{3,2,1,0:T(8,128)(2,1)S(1)} %copy-done.2, bf16[2,1,64,256]{3,2,1,0:T(8,128)(2,1)S(1)} %copy-done.3, ...), custom_call_target="tpu_custom_call" | custom-call | tf_op jit(solution)/shard_map/pallas_call | solution.py:319
  55.8 1.4 %copy.13 = f32[1,3,3,256,256]{4,3,2,1,0:T(8,128)} copy(f32[1,3,3,256,256]{4,3,2,1,0:T(8,128)S(1)} %get-tuple-element.6) | data formatting | bytes 4718592
  57.2 0.6 copy.14
  57.7 0.8 %copy.15 = f32[1,256,512]{2,1,0:T(8,128)} copy(f32[1,256,512]{2,1,0:T(8,128)S(1)} %get-tuple-element.8) | data formatting | bytes 1048576
Async XLA Ops:
  0.6 1.3 %copy-start = (bf16[1,3,3,256,256]{4,3,2,1,0:T(8,128)(2,1)S(1)}, bf16[1,3,3,256,256]{4,3,2,1,0:T(8,128)(2,1)}, u32[]{:S(2)}) copy-start(bf16[1,3,3,256,256]{4,3,2,1,0:T(8,128)(2,1)} %weight.1) | copy-start | bytes 3538948
  1.9 0.9 %copy-start.1 = (bf16[1,256,512]{2,1,0:T(8,128)(2,1)S(1)}, bf16[1,256,512]{2,1,0:T(8,128)(2,1)}, u32[]{:S(2)}) copy-start(bf16[1,256,512]{2,1,0:T(8,128)(2,1)} %emb.1) | copy-start | bytes 786436
  2.9 0.8 %copy-start.2 = (bf16[2,1,64,256]{3,2,1,0:T(8,128)(2,1)S(1)}, bf16[2,1,64,256]{3,2,1,0:T(8,128)(2,1)}, u32[]{:S(2)}) copy-start(bf16[2,1,64,256]{3,2,1,0:T(8,128)(2,1)} %images.1) | copy-start | bytes 196612
  3.7 0.8 %copy-start.3 = (bf16[2,1,64,256]{3,2,1,0:T(8,128)(2,1)S(1)}, bf16[2,1,64,256]{3,2,1,0:T(8,128)(2,1)}, u32[]{:S(2)}) copy-start(bf16[2,1,64,256]{3,2,1,0:T(8,128)(2,1)} %out_grad.1) | copy-start | bytes 196612
  4.5 0.7 %copy-start.4 = (f32[1,256]{1,0:T(1,128)S(1)}, f32[1,256]{1,0:T(1,128)}, u32[]{:S(2)}) copy-start(f32[1,256]{1,0:T(1,128)} %gain.1) | copy-start | bytes 3076
  5.2 0.7 %copy-start.5 = (s32[2]{0:T(128)S(1)}, s32[2]{0:T(128)}, u32[]{:S(2)}) copy-start(s32[2]{0:T(128)} %steps.1) | copy-start | bytes 28
  5.9 0.7 %copy-start.6 = (f32[1,128]{1,0:T(1,128)S(1)}, f32[1,128]{1,0:T(1,128)}, u32[]{:S(2)}) copy-start(f32[1,128]{1,0:T(1,128)} %constant.8.freqs) | copy-start | bytes 1540

commit v2 on v1

v2 whole, which is shorter than its diff:
```python
import functools
import math

import jax
import jax.numpy as jnp
import numpy as np
from jax import lax
from jax.experimental import pallas as pl
from jax.experimental.pallas import tpu as pltpu
from jax.sharding import PartitionSpec as P

G = 32
EPS = 1e-05
MESH = pl.DeviceIdType.MESH
F32 = jnp.float32
BF16 = jnp.bfloat16
PIX = 256
COLS = 64
C = 256
HALF = 128


def thirds(x):
    first = x.astype(BF16)
    rest = x - first.astype(F32)
    second = rest.astype(BF16)
    return first, second, (rest - second.astype(F32)).astype(BF16)


def exact_dot(x, matrix):
    parts = [jnp.dot(part, matrix, preferred_element_type=F32) for part in thirds(x)]
    return parts[0] + (parts[1] + parts[2])


def rows_of(*rows):
    index = lax.broadcasted_iota(jnp.int32, (8, rows[0].shape[1]), 0)
    out = jnp.zeros((8, rows[0].shape[1]), F32)
    for i, row in enumerate(rows):
        out = jnp.where(index == i, row, out)
    return out


def half_at(index):
    return pl.ds(pl.multiple_of(index * HALF, HALF), HALF)


def spread_columns(ref, value, half):
    column = lax.broadcasted_iota(jnp.int32, (PIX, HALF), 0) & (COLS - 1)
    left = jnp.where(column == 0, 0.0, pltpu.roll(value, 1, 0))
    right = jnp.where(column == COLS - 1, 0.0, pltpu.roll(value, PIX - 1, 0))
    for kx, moved in enumerate((left, value, right)):
        ref[COLS : COLS + PIX, half_at(2 * kx + half)] = moved.astype(BF16)


def clear_border(ref):
    blank = jnp.zeros((COLS, 3 * C), BF16)
    ref[0:COLS, :] = blank
    ref[COLS + PIX : 2 * COLS + PIX, :] = blank


def convolve(ref, kernel, half):
    total = None
    for ky in range(3):
        rows = slice(ky * COLS, ky * COLS + PIX)
        left = jnp.concatenate([ref[rows, half_at(2 * kx + half)] for kx in range(3)], axis=1)
        right = kernel[ky, :, half_at(half), :].reshape(3 * HALF, HALF)
        part = jnp.dot(left, right, preferred_element_type=F32)
        total = part if total is None else total + part
    return total


def chain_body(
    n_sec, flips, steps, freqs, images, out_grad, weight, gain, emb,
    act_out, cols_out, small_out,
    act_t, g_cols, small, hbuf, skip, gskip, obuf, dbuf, act_raw, g_all, plain, across, turned, act_cols,
    normed, slope, d_act, freqs_v, gain_v, emb_v, send, recv, local, leave,
):
    dp = lax.axis_index("dp")
    s = lax.axis_index("section")
    space = lax.axis_index("space")
    y = space // 2
    core = lax.rem(space, 2)
    last = n_sec - 1
    me = dp * 2 + y if len(flips) == 3 else y
    ahead, behind = lax.rem(s + 1, n_sec), lax.rem(s + n_sec - 1, n_sec)
    sibling = {"space": space ^ 1}

    def plane_peer(k, flip_core=0):
        return {"dp": dp ^ (k & 1), "space": space ^ (k & 2) ^ flip_core}

    others = [(k, f) for k in (0,) + flips for f in (0, 1) if k or f]
    barrier = pltpu.get_barrier_semaphore()
    partners = [plane_peer(k, f) if k & 1 else {"space": space ^ (k & 2) ^ f} for k, f in others]
    partners += [{"section": ahead}, {"section": behind}]
    for partner in partners:
        pl.semaphore_signal(barrier, inc=1, device_id=partner, device_id_type=MESH)

    loads = [
        pltpu.make_async_copy(src, dst, local.at[i])
        for i, (src, dst) in enumerate((
            (freqs, freqs_v),
            (emb.at[0, :, half_at(core)], emb_v.at[0]),
            (emb.at[0, :, half_at(core + 2)], emb_v.at[1]),
            (gain.at[:, half_at(core)], gain_v),
            (weight.at[0, :, :, :, half_at(core)], plain),
            (weight.at[0, :, :, half_at(core), :], across),
        ))
    ]
    for load in loads:
        load.start()

    def remote(src, dst, number, device):
        return pltpu.make_async_remote_copy(
            src_ref=src, dst_ref=dst, send_sem=send.at[number], recv_sem=recv.at[number],
            device_id=device, device_id_type=MESH,
        )

    def row_at(index):
        return pl.ds(pl.multiple_of(index * COLS, COLS), COLS)

    g_mine = g_all.at[me, core]
    g_cols_mine = g_cols.at[me]
    act_rows = half_at(core)

    def image_row(k):
        target = space ^ k
        return remote(
            images.at[target // 2, 0, :, half_at(lax.rem(target, 2))],
            hbuf.at[row_at(space), :], k - 1, {"space": target},
        )

    def grad_row(k):
        target = space ^ k
        return remote(
            out_grad.at[target // 2, 0, :, half_at(lax.rem(target, 2))],
            g_all.at[me ^ (k >> 1), lax.rem(target, 2), row_at(space), :],
            k - 1, {"space": target},
        )

    own_image = pltpu.make_async_copy(
        images.at[y, 0, :, half_at(core)], hbuf.at[row_at(space), :], local.at[6]
    )
    own_grad = pltpu.make_async_copy(
        out_grad.at[y, 0, :, half_at(core)], g_all.at[me, core, row_at(space), :], local.at[6]
    )
    forward_hop = remote(obuf, hbuf, 3, {"section": ahead})
    forward_skip = remote(obuf, skip, 4, {"section": behind})
    backward_hop = remote(dbuf, g_mine, 5, {"section": behind})
    backward_skip = remote(dbuf, gskip, 6, {"section": ahead})
    act_sibling = remote(act_raw.at[core], act_raw.at[core], 7, sibling)
    g_sibling = remote(g_mine, g_mine, 8, sibling)
    act_copy, g_copy, act_pass, g_pass, slot = {}, {}, {}, {}, {}
    for k in flips:
        slot[k] = me ^ (((k & 1) << 1) | (k >> 1))
        mine = act_t.at[me, act_rows, :]
        theirs = act_t.at[slot[k], act_rows, :]
        act_copy[k] = remote(mine, mine, 8 + k, plane_peer(k))
        g_copy[k] = remote(g_mine, g_mine, 11 + k, plane_peer(k))
        act_pass[k] = remote(theirs, theirs, 14 + k, sibling)
        passed = g_all.at[slot[k], core]
        g_pass[k] = remote(passed, passed, 17 + k, sibling)
    small_copy = [
        remote(small.at[me, core], small.at[me, core], 21 + i, plane_peer(k, f))
        for i, (k, f) in enumerate(others)
    ]

    clear_border(act_cols)
    for i in range(4):
        clear_border(g_cols.at[i])
    same = (
        lax.broadcasted_iota(jnp.int32, (HALF, HALF), 0) // (C // G)
        == lax.broadcasted_iota(jnp.int32, (HALF, HALF), 1) // (C // G)
    ).astype(F32).astype(BF16)
    cells = PIX * (C // G)

    pl.semaphore_wait(barrier, len(partners))

    @pl.when(s == 0)
    def _():
        for k in (1, 2, 3):
            image_row(k).start()
        own_image.start()

    @pl.when(s == last)
    def _():
        for k in (1, 2, 3):
            grad_row(k).start()
        own_grad.start()

    for load in loads[:4]:
        load.wait()
    angles = steps[y].astype(F32) * freqs_v[...]
    cosines, sines = jnp.cos(angles), jnp.sin(angles)
    features = jnp.broadcast_to(jnp.concatenate([cosines, sines], axis=1), (8, C))
    scales1 = 1.0 + exact_dot(features, emb_v[0])[0:1]
    shifts = exact_dot(features, emb_v[1])[0:1]
    gains = gain_v[...]
    factor = gains * scales1
    for load in loads[4:]:
        load.wait()

    def turn_weights():
        for ky in range(3):
            for kx in range(3):
                turned[ky, kx] = across[2 - ky, 2 - kx].T

    def back_convolve():
        g_sibling.start()
        for k in flips:
            g_copy[k].start()
        spread_columns(g_cols_mine, g_mine[...].astype(F32), core)
        total = convolve(g_cols_mine, turned, core)
        g_sibling.wait_recv()
        spread_columns(g_cols_mine, g_all[me, 1 - core].astype(F32), 1 - core)
        d_act[...] = total + convolve(g_cols_mine, turned, 1 - core)

    @pl.when(s == 0)
    def _():
        own_image.wait()
        for k in (1, 2, 3):
            image_row(k).wait_recv()

    @pl.when(s == last)
    def _():
        turn_weights()
        own_grad.wait()
        for k in (1, 2, 3):
            grad_row(k).wait_recv()
        back_convolve()

    @pl.when(s > 0)
    def _():
        forward_hop.wait_recv()

    @pl.when(s == last)
    def _():
        forward_skip.wait_recv()
        hbuf[...] = (hbuf[...].astype(F32) + skip[...].astype(F32)).astype(BF16)

    tensor = hbuf[...].astype(F32)
    first = jnp.sum(tensor, axis=0, keepdims=True)
    square = jnp.sum(tensor * tensor, axis=0, keepdims=True)
    sums = exact_dot(rows_of(first, square), same) * (1.0 / cells)
    average = sums[0:1]
    inverse = lax.rsqrt(sums[1:2] - average * average + EPS)
    normal = (tensor - average) * inverse
    normed[...] = normal
    pre = normal * factor + shifts
    sigmoid = jax.nn.sigmoid(pre)
    act = pre * sigmoid
    act_raw[core] = act.astype(BF16)
    act_sibling.start()

    @pl.when(s < last)
    def _():
        spread_columns(act_cols, act, core)
        out = hbuf[...].astype(F32) + convolve(act_cols, plain, core)
        act_sibling.wait_recv()
        spread_columns(act_cols, act_raw[1 - core].astype(F32), 1 - core)
        obuf[...] = (out + convolve(act_cols, plain, 1 - core)).astype(BF16)
        forward_hop.start()

    @pl.when(s == 0)
    def _():
        forward_skip.start()

    slope[...] = sigmoid * (1.0 + pre * (1.0 - sigmoid))

    def share_act():
        act_t[me, act_rows, :] = act_raw[core].T
        for k in flips:
            act_copy[k].start()
        act_t[me, half_at(1 - core), :] = act_raw[1 - core].T

    @pl.when(s < last)
    def _():
        share_act()
        turn_weights()
        backward_hop.wait_recv()

    @pl.when(s == 0)
    def _():
        backward_skip.wait_recv()
        g_all[me, core] = (g_mine[...].astype(F32) + gskip[...].astype(F32)).astype(BF16)

    @pl.when(s < last)
    def _():
        back_convolve()

    d_pre = d_act[...] * slope[...]
    normal = normed[...]
    sum_pre = jnp.sum(d_pre, axis=0, keepdims=True)
    sum_normal = jnp.sum(d_pre * normal, axis=0, keepdims=True)

    @pl.when(s > 0)
    def _():
        means = exact_dot(rows_of(sum_pre * factor, sum_normal * factor), same) * (1.0 / cells)
        d_tensor = inverse * (d_pre * factor - means[0:1] - normal * means[1:2])
        dbuf[...] = (g_mine[...].astype(F32) + d_tensor).astype(BF16)
        backward_hop.start()

    @pl.when(s == last)
    def _():
        backward_skip.start()
        act_sibling.wait_recv()
        share_act()

    small[me, core] = rows_of(sum_normal * gains, sum_pre, sum_normal * scales1, cosines, sines)
    for copy in small_copy:
        copy.start()

    def image_out(slot_no, number):
        return [
            pltpu.make_async_copy(act_t.at[slot_no], act_out.at[slot_no], leave.at[number]),
            pltpu.make_async_copy(g_cols.at[slot_no], cols_out.at[slot_no], leave.at[4 + number]),
        ]

    leaving = image_out(me, 0)
    for copy in leaving:
        copy.start()

    for k in flips:
        act_copy[k].wait_recv()
        act_pass[k].start()
    for k in flips:
        g_copy[k].wait_recv()
        g_pass[k].start()
        spread_columns(g_cols.at[slot[k]], g_all[slot[k], core].astype(F32), core)
    for k in flips:
        act_pass[k].wait_recv()
        g_pass[k].wait_recv()
        spread_columns(g_cols.at[slot[k]], g_all[slot[k], 1 - core].astype(F32), 1 - core)
        for copy in image_out(slot[k], k):
            copy.start()
            leaving.append(copy)
    for copy in small_copy:
        copy.wait_recv()
    leaving.append(pltpu.make_async_copy(small, small_out, leave.at[8]))
    leaving[-1].start()

    @pl.when(s == 0)
    def _():
        for k in (1, 2, 3):
            image_row(k).wait_send()
        forward_skip.wait_send()

    @pl.when(s == last)
    def _():
        for k in (1, 2, 3):
            grad_row(k).wait_send()
        backward_skip.wait_send()

    @pl.when(s < last)
    def _():
        forward_hop.wait_send()

    @pl.when(s > 0)
    def _():
        backward_hop.wait_send()

    act_sibling.wait_send()
    g_sibling.wait_send()
    for k in flips:
        for copy in (act_copy[k], g_copy[k], act_pass[k], g_pass[k]):
            copy.wait_send()
    for copy in small_copy:
        copy.wait_send()
    for copy in leaving:
        copy.wait()


def grad_body(
    slots, act_in, cols_in, small_in, conv_out, gain_out, emb_out,
    act_t, g_cols, small, taps, gain_v, emb_v, sems,
):
    loads = [pltpu.make_async_copy(small_in, small, sems.at[11])]
    for i in range(slots):
        loads.append(pltpu.make_async_copy(act_in.at[i], act_t.at[i], sems.at[12 + i]))
        loads.append(pltpu.make_async_copy(cols_in.at[i], g_cols.at[i], sems.at[16 + i]))
    for load in loads:
        load.start()
    loads[0].wait()
    packed = [jnp.concatenate([small[i, 0], small[i, 1]], axis=1) for i in range(slots)]
    gain_total = packed[0][2:3]
    for block in packed[1:]:
        gain_total = gain_total + block[2:3]
    gain_v[...] = gain_total
    features = rows_of(
        *[jnp.concatenate([small[i, 0, 3:4], small[i, 0, 4:5]], axis=1) for i in range(slots)]
    )
    d_rows = rows_of(*[jnp.concatenate([block[0:1], block[1:2]], axis=1) for block in packed])
    emb_v[...] = jnp.dot(
        features.T, d_rows, precision=lax.Precision.HIGHEST, preferred_element_type=F32
    )
    copies = [
        pltpu.make_async_copy(gain_v, gain_out, sems.at[9]),
        pltpu.make_async_copy(emb_v, emb_out.at[0], sems.at[10]),
    ]
    for copy in copies:
        copy.start()
    for load in loads[1:]:
        load.wait()
    for ky in range(3):
        for kx in range(3):
            total = None
            for i in range(slots):
                piece = jnp.dot(
                    act_t[i],
                    g_cols[i, ky * COLS : ky * COLS + PIX, kx * C : (kx + 1) * C],
                    preferred_element_type=F32,
                )
                total = piece if total is None else total + piece
            tap = ky * 3 + kx
            taps[tap] = total
            copy = pltpu.make_async_copy(taps.at[tap], conv_out.at[0, 2 - ky, 2 - kx], sems.at[tap])
            copy.start()
            copies.append(copy)
    for copy in copies:
        copy.wait()


def per_device(images, steps, out_grad, conv_weight, gn_gain, emb_weight):
    n_dp = lax.axis_size("dp")
    n_sec = lax.axis_size("section")
    flips = (1, 2, 3) if n_dp == 2 else (2,)
    half = C // 2
    freqs = np.exp(-math.log(10000.0) * np.arange(half, dtype=np.float32) / half)
    hbm = pl.BlockSpec(memory_space=pltpu.HBM)
    padded = PIX + 2 * COLS
    chain = pl.pallas_call(
        functools.partial(chain_body, n_sec, flips),
        out_shape=(
            jax.ShapeDtypeStruct((4, C, PIX), BF16),
            jax.ShapeDtypeStruct((4, padded, 3 * C), BF16),
            jax.ShapeDtypeStruct((4, 2, 8, HALF), F32),
        ),
        in_specs=[pl.BlockSpec(memory_space=pltpu.SMEM)] + [hbm] * 6,
        out_specs=(hbm, hbm, hbm),
        scratch_shapes=[
            pltpu.VMEM((4, C, PIX), BF16),
            pltpu.VMEM((4, padded, 3 * C), BF16),
            pltpu.VMEM((4, 2, 8, HALF), F32),
            pltpu.VMEM((PIX, HALF), BF16),
            pltpu.VMEM((PIX, HALF), BF16),
            pltpu.VMEM((PIX, HALF), BF16),
            pltpu.VMEM((PIX, HALF), BF16),
            pltpu.VMEM((PIX, HALF), BF16),
            pltpu.VMEM((2, PIX, HALF), BF16),
            pltpu.VMEM((4, 2, PIX, HALF), BF16),
            pltpu.VMEM((3, 3, C, HALF), BF16),
            pltpu.VMEM((3, 3, HALF, C), BF16),
            pltpu.VMEM((3, 3, C, HALF), BF16),
            pltpu.VMEM((padded, 3 * C), BF16),
            pltpu.VMEM((PIX, HALF), F32),
            pltpu.VMEM((PIX, HALF), F32),
            pltpu.VMEM((PIX, HALF), F32),
            pltpu.VMEM((1, HALF), F32),
            pltpu.VMEM((1, HALF), F32),
            pltpu.VMEM((2, C, HALF), BF16),
            pltpu.SemaphoreType.DMA((28,)),
            pltpu.SemaphoreType.DMA((28,)),
            pltpu.SemaphoreType.DMA((7,)),
            pltpu.SemaphoreType.DMA((9,)),
        ],
        compiler_params=pltpu.CompilerParams(
            collective_id=0, has_side_effects=True, vmem_limit_bytes=56 * 1024 * 1024
        ),
    )(
        steps, jnp.asarray(freqs, F32)[None, :], images, out_grad, conv_weight, gn_gain, emb_weight
    )
    grads = pl.pallas_call(
        functools.partial(grad_body, 4 if n_dp == 2 else 2),
        out_shape=(
            jax.ShapeDtypeStruct((1, 3, 3, C, C), F32),
            jax.ShapeDtypeStruct((1, C), F32),
            jax.ShapeDtypeStruct((1, C, 2 * C), F32),
        ),
        in_specs=[hbm] * 3,
        out_specs=(hbm, hbm, hbm),
        scratch_shapes=[
            pltpu.VMEM((4, C, PIX), BF16),
            pltpu.VMEM((4, padded, 3 * C), BF16),
            pltpu.VMEM((4, 2, 8, HALF), F32),
            pltpu.VMEM((9, C, C), F32),
            pltpu.VMEM((1, C), F32),
            pltpu.VMEM((C, 2 * C), F32),
            pltpu.SemaphoreType.DMA((20,)),
        ],
        compiler_params=pltpu.CompilerParams(vmem_limit_bytes=56 * 1024 * 1024),
    )(*chain)
    if n_dp != 2:
        grads = lax.psum(grads, "dp")
    return grads


def solution(mesh):
    in_specs = (
        P("dp", "space", None, None),
        P("dp"),
        P("dp", "space", None, None),
        P("section", None, None, None, None),
        P("section", None),
        P("section", None, None),
    )
    out_specs = (P("section", None, None, None, None), P("section", None), P("section", None, None))
    return jax.shard_map(
        per_device, mesh=mesh, in_specs=in_specs, out_specs=out_specs, check_vma=False
    )
```

time: 58.8 us -> 51.1 us (0.87)
  local copies, waits for them, and re-layouts: 8.64 us -> 0 us
  Pallas kernels: 49.2 us -> 50 us
    unnamed x17 -> x0, local copies, waits for them, and re-layouts: 8.64 us -> none
    pallas_call x1 -> x2, Pallas kernels: 49.2 us -> 50 us  [the longest x1 45.8 us: per_device(): pl.pallas_call(functools.partial(chain_body, n_sec, flips), out_shape=(ja...]
where the time goes in v2:
time: 51.1 us; the launch traced here: 50.6 us
  Pallas kernels  50 us (98%)
  between operations  0.64 us (1%)
    pallas_call x1, Pallas kernels, per_device(): pl.pallas_call(functools.partial(chain_body, n_sec, flips), out_shape=(ja...  45.8 us
    pallas_call x1, Pallas kernels, per_device(): pl.pallas_call(functools.partial(grad_body, 4 if n_dp == 2 else 2), out_s...  4.21 us

profile of v2, /device:TPU:0, one launch (start us, length us, event | category | flops | bytes accessed | tf_op | source)
XLA Modules:
  0.0 50.6 jit_solution(8197101160770192894)
XLA Ops:
  0.6 45.8 %shard_map.94 = (bf16[4,256,256]{2,1,0:T(8,128)(2,1)}, bf16[4,384,768]{2,1,0:T(8,128)(2,1)}, f32[4,2,8,128]{3,2,1,0:T(8,128)}) custom-call(s32[2]{0:T(128)} %steps.1, f32[1,128]{1,0:T(1,128)} %constant.8.freqs, bf16[2,1,64,256]{3,2,1,0:T(8,128)(2,1)} %images.1, bf16[2,1,64,256]{3,2,1,0:T(8,128)(2,1)} %out_grad.1, bf16[1,3,3,256,256]{4,3,2,1,0:T(8,128)(2,1)} %weight.1, ...), custom_call_target="tpu_custom_call" | custom-call | tf_op jit(solution)/shard_map/pallas_call | solution.py:430
  46.4 4.2 %shard_map.95 = (f32[1,3,3,256,256]{4,3,2,1,0:T(8,128)}, f32[1,256]{1,0:T(1,128)}, f32[1,256,512]{2,1,0:T(8,128)}) custom-call(bf16[4,256,256]{2,1,0:T(8,128)(2,1)} %get-tuple-element.6.act_in, bf16[4,384,768]{2,1,0:T(8,128)(2,1)} %get-tuple-element.7.cols_in, f32[4,2,8,128]{3,2,1,0:T(8,128)} %get-tuple-element.8.small_in), custom_call_target="tpu_custom_call" | custom-call | tf_op jit(solution)/shard_map/pallas_call | solution.py:471

commit v3 on v2

--- a/solution.py
+++ b/solution.py
@@ -44,6 +44,12 @@
     return pl.ds(pl.multiple_of(index * HALF, HALF), HALF)
 
 
+def group_means(first, second, same, scale):
+    parts = [p.astype(F32) for p in thirds(first) + thirds(second)]
+    sums = jnp.dot(rows_of(*parts).astype(BF16), same, preferred_element_type=F32) * scale
+    return sums[0:1] + (sums[1:2] + sums[2:3]), sums[3:4] + (sums[4:5] + sums[5:6])
+
+
 def spread_columns(ref, value, half):
     column = lax.broadcasted_iota(jnp.int32, (PIX, HALF), 0) & (COLS - 1)
     left = jnp.where(column == 0, 0.0, pltpu.roll(value, 1, 0))
@@ -58,15 +64,17 @@
     ref[COLS + PIX : 2 * COLS + PIX, :] = blank
 
 
-def convolve(ref, kernel, half):
-    total = None
-    for ky in range(3):
-        rows = slice(ky * COLS, ky * COLS + PIX)
-        left = jnp.concatenate([ref[rows, half_at(2 * kx + half)] for kx in range(3)], axis=1)
-        right = kernel[ky, :, half_at(half), :].reshape(3 * HALF, HALF)
-        part = jnp.dot(left, right, preferred_element_type=F32)
-        total = part if total is None else total + part
-    return total
+def convolve(ref, kernel, half, start=0, count=PIX):
+    left = jnp.concatenate(
+        [
+            ref[ky * COLS + start : ky * COLS + start + count, half_at(2 * kx + half)]
+            for ky in range(3)
+            for kx in range(3)
+        ],
+        axis=1,
+    )
+    right = kernel[:, :, half_at(half), :].reshape(9 * HALF, HALF)
+    return jnp.dot(left, right, preferred_element_type=F32)
 
 
 def chain_body(
@@ -143,7 +151,11 @@
     own_grad = pltpu.make_async_copy(
         out_grad.at[y, 0, :, half_at(core)], g_all.at[me, core, row_at(space), :], local.at[6]
     )
-    forward_hop = remote(obuf, hbuf, 3, {"section": ahead})
+    pieces = [slice(0, PIX // 2), slice(PIX // 2, PIX)]
+    forward_hop = [
+        remote(obuf.at[piece, :], hbuf.at[piece, :], number, {"section": ahead})
+        for piece, number in zip(pieces, (3, 28))
+    ]
     forward_skip = remote(obuf, skip, 4, {"section": behind})
     backward_hop = remote(dbuf, g_mine, 5, {"section": behind})
     backward_skip = remote(dbuf, gskip, 6, {"section": ahead})
@@ -206,8 +218,6 @@
 
     def back_convolve():
         g_sibling.start()
-        for k in flips:
-            g_copy[k].start()
         spread_columns(g_cols_mine, g_mine[...].astype(F32), core)
         total = convolve(g_cols_mine, turned, core)
         g_sibling.wait_recv()
@@ -230,7 +240,8 @@
 
     @pl.when(s > 0)
     def _():
-        forward_hop.wait_recv()
+        for hop in forward_hop:
+            hop.wait_recv()
 
     @pl.when(s == last)
     def _():
@@ -240,9 +251,8 @@
     tensor = hbuf[...].astype(F32)
     first = jnp.sum(tensor, axis=0, keepdims=True)
     square = jnp.sum(tensor * tensor, axis=0, keepdims=True)
-    sums = exact_dot(rows_of(first, square), same) * (1.0 / cells)
-    average = sums[0:1]
-    inverse = lax.rsqrt(sums[1:2] - average * average + EPS)
+    average, mean_square = group_means(first, square, same, 1.0 / cells)
+    inverse = lax.rsqrt(mean_square - average * average + EPS)
     normal = (tensor - average) * inverse
     normed[...] = normal
     pre = normal * factor + shifts
@@ -257,8 +267,10 @@
         out = hbuf[...].astype(F32) + convolve(act_cols, plain, core)
         act_sibling.wait_recv()
         spread_columns(act_cols, act_raw[1 - core].astype(F32), 1 - core)
-        obuf[...] = (out + convolve(act_cols, plain, 1 - core)).astype(BF16)
-        forward_hop.start()
+        for piece, hop in zip(pieces, forward_hop):
+            more = convolve(act_cols, plain, 1 - core, piece.start, PIX // 2)
+            obuf[piece, :] = (out[piece] + more).astype(BF16)
+            hop.start()
 
     @pl.when(s == 0)
     def _():
@@ -283,6 +295,14 @@
         backward_skip.wait_recv()
         g_all[me, core] = (g_mine[...].astype(F32) + gskip[...].astype(F32)).astype(BF16)
 
+    def share_grad():
+        for k in reversed(flips):
+            g_copy[k].start()
+
+    @pl.when(s == 0)
+    def _():
+        share_grad()
+
     @pl.when(s < last)
     def _():
         back_convolve()
@@ -294,10 +314,11 @@
 
     @pl.when(s > 0)
     def _():
-        means = exact_dot(rows_of(sum_pre * factor, sum_normal * factor), same) * (1.0 / cells)
-        d_tensor = inverse * (d_pre * factor - means[0:1] - normal * means[1:2])
+        mean_d, mean_dn = group_means(sum_pre * factor, sum_normal * factor, same, 1.0 / cells)
+        d_tensor = inverse * (d_pre * factor - mean_d - normal * mean_dn)
         dbuf[...] = (g_mine[...].astype(F32) + d_tensor).astype(BF16)
         backward_hop.start()
+        share_grad()
 
     @pl.when(s == last)
     def _():
@@ -352,7 +373,8 @@
 
     @pl.when(s < last)
     def _():
-        forward_hop.wait_send()
+        for hop in forward_hop:
+            hop.wait_send()
 
     @pl.when(s > 0)
     def _():
@@ -376,8 +398,16 @@
     loads = [pltpu.make_async_copy(small_in, small, sems.at[11])]
     for i in range(slots):
         loads.append(pltpu.make_async_copy(act_in.at[i], act_t.at[i], sems.at[12 + i]))
-        loads.append(pltpu.make_async_copy(cols_in.at[i], g_cols.at[i], sems.at[16 + i]))
-    for load in loads:
+    shifted = []
+    for kx in range(3):
+        lanes = slice(kx * C, (kx + 1) * C)
+        shifted.append([
+            pltpu.make_async_copy(
+                cols_in.at[i, :, lanes], g_cols.at[i, :, lanes], sems.at[16 + 4 * kx + i]
+            )
+            for i in range(slots)
+        ])
+    for load in loads + shifted[0] + shifted[1] + shifted[2]:
         load.start()
     loads[0].wait()
     packed = [jnp.concatenate([small[i, 0], small[i, 1]], axis=1) for i in range(slots)]
@@ -400,8 +430,10 @@
         copy.start()
     for load in loads[1:]:
         load.wait()
-    for ky in range(3):
-        for kx in range(3):
+    for kx in range(3):
+        for load in shifted[kx]:
+            load.wait()
+        for ky in range(3):
             total = None
             for i in range(slots):
                 piece = jnp.dot(
@@ -457,8 +489,8 @@
             pltpu.VMEM((1, HALF), F32),
             pltpu.VMEM((1, HALF), F32),
             pltpu.VMEM((2, C, HALF), BF16),
-            pltpu.SemaphoreType.DMA((28,)),
-            pltpu.SemaphoreType.DMA((28,)),
+            pltpu.SemaphoreType.DMA((29,)),
+            pltpu.SemaphoreType.DMA((29,)),
             pltpu.SemaphoreType.DMA((7,)),
             pltpu.SemaphoreType.DMA((9,)),
         ],
@@ -484,7 +516,7 @@
             pltpu.VMEM((9, C, C), F32),
             pltpu.VMEM((1, C), F32),
             pltpu.VMEM((C, 2 * C), F32),
-            pltpu.SemaphoreType.DMA((20,)),
+            pltpu.SemaphoreType.DMA((28,)),
         ],
         compiler_params=pltpu.CompilerParams(vmem_limit_bytes=56 * 1024 * 1024),
     )(*chain)

time: 51.1 us -> 51.4 us (level)
  no operation moved by 1% of the time
where the time goes in v3:
time: 51.4 us; the launch traced here: 50.6 us
  Pallas kernels  49.9 us (97%)
  between operations  0.64 us (1%)
    pallas_call x1, Pallas kernels, per_device(): pl.pallas_call(functools.partial(chain_body, n_sec, flips), out_shape=(ja...  45.3 us
    pallas_call x1, Pallas kernels, per_device(): pl.pallas_call(functools.partial(grad_body, 4 if n_dp == 2 else 2), out_s...  4.62 us

profile of v3, /device:TPU:0, one launch (start us, length us, event | category | flops | bytes accessed | tf_op | source)
XLA Modules:
  0.0 50.6 jit_solution(8755298135587529963)
XLA Ops:
  0.6 45.3 %shard_map.94 = (bf16[4,256,256]{2,1,0:T(8,128)(2,1)}, bf16[4,384,768]{2,1,0:T(8,128)(2,1)}, f32[4,2,8,128]{3,2,1,0:T(8,128)}) custom-call(s32[2]{0:T(128)} %steps.1, f32[1,128]{1,0:T(1,128)} %constant.8.freqs, bf16[2,1,64,256]{3,2,1,0:T(8,128)(2,1)} %images.1, bf16[2,1,64,256]{3,2,1,0:T(8,128)(2,1)} %out_grad.1, bf16[1,3,3,256,256]{4,3,2,1,0:T(8,128)(2,1)} %weight.1, ...), custom_call_target="tpu_custom_call" | custom-call | tf_op jit(solution)/shard_map/pallas_call | solution.py:462
  46.0 4.6 %shard_map.95 = (f32[1,3,3,256,256]{4,3,2,1,0:T(8,128)}, f32[1,256]{1,0:T(1,128)}, f32[1,256,512]{2,1,0:T(8,128)}) custom-call(bf16[4,256,256]{2,1,0:T(8,128)(2,1)} %get-tuple-element.6.act_in, bf16[4,384,768]{2,1,0:T(8,128)(2,1)} %get-tuple-element.7.cols_in, f32[4,2,8,128]{3,2,1,0:T(8,128)} %get-tuple-element.8.small_in), custom_call_target="tpu_custom_call" | custom-call | tf_op jit(solution)/shard_map/pallas_call | solution.py:503

commit v4 on v2

--- a/solution.py
+++ b/solution.py
@@ -27,11 +27,6 @@
     return first, second, (rest - second.astype(F32)).astype(BF16)
 
 
-def exact_dot(x, matrix):
-    parts = [jnp.dot(part, matrix, preferred_element_type=F32) for part in thirds(x)]
-    return parts[0] + (parts[1] + parts[2])
-
-
 def rows_of(*rows):
     index = lax.broadcasted_iota(jnp.int32, (8, rows[0].shape[1]), 0)
     out = jnp.zeros((8, rows[0].shape[1]), F32)
@@ -44,6 +39,12 @@
     return pl.ds(pl.multiple_of(index * HALF, HALF), HALF)
 
 
+def group_means(first, second, same, scale):
+    parts = [p.astype(F32) for p in thirds(first) + thirds(second)]
+    sums = jnp.dot(rows_of(*parts).astype(BF16), same, preferred_element_type=F32) * scale
+    return sums[0:1] + (sums[1:2] + sums[2:3]), sums[3:4] + (sums[4:5] + sums[5:6])
+
+
 def spread_columns(ref, value, half):
     column = lax.broadcasted_iota(jnp.int32, (PIX, HALF), 0) & (COLS - 1)
     left = jnp.where(column == 0, 0.0, pltpu.roll(value, 1, 0))
@@ -59,21 +60,23 @@
 
 
 def convolve(ref, kernel, half):
-    total = None
-    for ky in range(3):
-        rows = slice(ky * COLS, ky * COLS + PIX)
-        left = jnp.concatenate([ref[rows, half_at(2 * kx + half)] for kx in range(3)], axis=1)
-        right = kernel[ky, :, half_at(half), :].reshape(3 * HALF, HALF)
-        part = jnp.dot(left, right, preferred_element_type=F32)
-        total = part if total is None else total + part
-    return total
+    left = jnp.concatenate(
+        [
+            ref[ky * COLS : ky * COLS + PIX, half_at(2 * kx + half)]
+            for ky in range(3)
+            for kx in range(3)
+        ],
+        axis=1,
+    )
+    right = kernel[:, :, half_at(half), :].reshape(9 * HALF, HALF)
+    return jnp.dot(left, right, preferred_element_type=F32)
 
 
 def chain_body(
     n_sec, flips, steps, freqs, images, out_grad, weight, gain, emb,
     act_out, cols_out, small_out,
     act_t, g_cols, small, hbuf, skip, gskip, obuf, dbuf, act_raw, g_all, plain, across, turned, act_cols,
-    normed, slope, d_act, freqs_v, gain_v, emb_v, send, recv, local, leave,
+    normed, slope, d_act, steps_v, freqs_v, gain_v, emb_v, send, recv, local, leave,
 ):
     dp = lax.axis_index("dp")
     s = lax.axis_index("section")
@@ -98,6 +101,7 @@
     loads = [
         pltpu.make_async_copy(src, dst, local.at[i])
         for i, (src, dst) in enumerate((
+            (steps, steps_v),
             (freqs, freqs_v),
             (emb.at[0, :, half_at(core)], emb_v.at[0]),
             (emb.at[0, :, half_at(core + 2)], emb_v.at[1]),
@@ -138,10 +142,10 @@
         )
 
     own_image = pltpu.make_async_copy(
-        images.at[y, 0, :, half_at(core)], hbuf.at[row_at(space), :], local.at[6]
+        images.at[y, 0, :, half_at(core)], hbuf.at[row_at(space), :], local.at[7]
     )
     own_grad = pltpu.make_async_copy(
-        out_grad.at[y, 0, :, half_at(core)], g_all.at[me, core, row_at(space), :], local.at[6]
+        out_grad.at[y, 0, :, half_at(core)], g_all.at[me, core, row_at(space), :], local.at[7]
     )
     forward_hop = remote(obuf, hbuf, 3, {"section": ahead})
     forward_skip = remote(obuf, skip, 4, {"section": behind})
@@ -164,6 +168,22 @@
         for i, (k, f) in enumerate(others)
     ]
 
+    for load in loads[:5]:
+        load.wait()
+    angles = steps_v[y].astype(F32) * freqs_v[...]
+    cosines, sines = jnp.cos(angles), jnp.sin(angles)
+    features = jnp.concatenate([cosines, sines], axis=1)
+    features = rows_of(*[p.astype(F32) for p in thirds(features)]).astype(BF16)
+    scales1, shifts = (
+        part[0:1] + (part[1:2] + part[2:3])
+        for part in (
+            jnp.dot(features, emb_v[i], preferred_element_type=F32) for i in range(2)
+        )
+    )
+    scales1 = 1.0 + scales1
+    gains = gain_v[...]
+    factor = gains * scales1
+
     clear_border(act_cols)
     for i in range(4):
         clear_border(g_cols.at[i])
@@ -187,16 +207,7 @@
             grad_row(k).start()
         own_grad.start()
 
-    for load in loads[:4]:
-        load.wait()
-    angles = steps[y].astype(F32) * freqs_v[...]
-    cosines, sines = jnp.cos(angles), jnp.sin(angles)
-    features = jnp.broadcast_to(jnp.concatenate([cosines, sines], axis=1), (8, C))
-    scales1 = 1.0 + exact_dot(features, emb_v[0])[0:1]
-    shifts = exact_dot(features, emb_v[1])[0:1]
-    gains = gain_v[...]
-    factor = gains * scales1
-    for load in loads[4:]:
+    for load in loads[5:]:
         load.wait()
 
     def turn_weights():
@@ -206,8 +217,6 @@
 
     def back_convolve():
         g_sibling.start()
-        for k in flips:
-            g_copy[k].start()
         spread_columns(g_cols_mine, g_mine[...].astype(F32), core)
         total = convolve(g_cols_mine, turned, core)
         g_sibling.wait_recv()
@@ -240,9 +249,8 @@
     tensor = hbuf[...].astype(F32)
     first = jnp.sum(tensor, axis=0, keepdims=True)
     square = jnp.sum(tensor * tensor, axis=0, keepdims=True)
-    sums = exact_dot(rows_of(first, square), same) * (1.0 / cells)
-    average = sums[0:1]
-    inverse = lax.rsqrt(sums[1:2] - average * average + EPS)
+    average, mean_square = group_means(first, square, same, 1.0 / cells)
+    inverse = lax.rsqrt(mean_square - average * average + EPS)
     normal = (tensor - average) * inverse
     normed[...] = normal
     pre = normal * factor + shifts
@@ -283,6 +291,14 @@
         backward_skip.wait_recv()
         g_all[me, core] = (g_mine[...].astype(F32) + gskip[...].astype(F32)).astype(BF16)
 
+    def share_grad():
+        for k in reversed(flips):
+            g_copy[k].start()
+
+    @pl.when(s == 0)
+    def _():
+        share_grad()
+
     @pl.when(s < last)
     def _():
         back_convolve()
@@ -294,10 +310,11 @@
 
     @pl.when(s > 0)
     def _():
-        means = exact_dot(rows_of(sum_pre * factor, sum_normal * factor), same) * (1.0 / cells)
-        d_tensor = inverse * (d_pre * factor - means[0:1] - normal * means[1:2])
+        mean_d, mean_dn = group_means(sum_pre * factor, sum_normal * factor, same, 1.0 / cells)
+        d_tensor = inverse * (d_pre * factor - mean_d - normal * mean_dn)
         dbuf[...] = (g_mine[...].astype(F32) + d_tensor).astype(BF16)
         backward_hop.start()
+        share_grad()
 
     @pl.when(s == last)
     def _():
@@ -400,16 +417,12 @@
         copy.start()
     for load in loads[1:]:
         load.wait()
+    left = jnp.concatenate([act_t[i] for i in range(slots)], axis=1)
     for ky in range(3):
         for kx in range(3):
-            total = None
-            for i in range(slots):
-                piece = jnp.dot(
-                    act_t[i],
-                    g_cols[i, ky * COLS : ky * COLS + PIX, kx * C : (kx + 1) * C],
-                    preferred_element_type=F32,
-                )
-                total = piece if total is None else total + piece
+            rows, lanes = slice(ky * COLS, ky * COLS + PIX), slice(kx * C, (kx + 1) * C)
+            right = jnp.concatenate([g_cols[i, rows, lanes] for i in range(slots)], axis=0)
+            total = jnp.dot(left, right, preferred_element_type=F32)
             tap = ky * 3 + kx
             taps[tap] = total
             copy = pltpu.make_async_copy(taps.at[tap], conv_out.at[0, 2 - ky, 2 - kx], sems.at[tap])
@@ -434,7 +447,7 @@
             jax.ShapeDtypeStruct((4, padded, 3 * C), BF16),
             jax.ShapeDtypeStruct((4, 2, 8, HALF), F32),
         ),
-        in_specs=[pl.BlockSpec(memory_space=pltpu.SMEM)] + [hbm] * 6,
+        in_specs=[hbm] * 7,
         out_specs=(hbm, hbm, hbm),
         scratch_shapes=[
             pltpu.VMEM((4, C, PIX), BF16),
@@ -454,12 +467,13 @@
             pltpu.VMEM((PIX, HALF), F32),
             pltpu.VMEM((PIX, HALF), F32),
             pltpu.VMEM((PIX, HALF), F32),
+            pltpu.SMEM((2,), jnp.int32),
             pltpu.VMEM((1, HALF), F32),
             pltpu.VMEM((1, HALF), F32),
             pltpu.VMEM((2, C, HALF), BF16),
             pltpu.SemaphoreType.DMA((28,)),
             pltpu.SemaphoreType.DMA((28,)),
-            pltpu.SemaphoreType.DMA((7,)),
+            pltpu.SemaphoreType.DMA((8,)),
             pltpu.SemaphoreType.DMA((9,)),
         ],
         compiler_params=pltpu.CompilerParams(

time: 51.1 us -> 50.8 us (level)
  Pallas kernels: 50 us -> 49.3 us
    pallas_call x1, Pallas kernels: 45.8 us -> 45.1 us  [per_device(): pl.pallas_call(functools.partial(chain_body, n_sec, flips), out_shape=(ja...]
where the time goes in v4:
time: 50.8 us; the launch traced here: 49.9 us
  Pallas kernels  49.3 us (97%)
  between operations  0.64 us (1%)
    pallas_call x1, Pallas kernels, per_device(): pl.pallas_call(functools.partial(chain_body, n_sec, flips), out_shape=(ja...  45.1 us
    pallas_call x1, Pallas kernels, per_device(): pl.pallas_call(functools.partial(grad_body, 4 if n_dp == 2 else 2), out_s...  4.21 us

profile of v4, /device:TPU:0, one launch (start us, length us, event | category | flops | bytes accessed | tf_op | source)
XLA Modules:
  0.0 49.9 jit_solution(7750134679684627567)
XLA Ops:
  0.6 45.1 %shard_map.94 = (bf16[4,256,256]{2,1,0:T(8,128)(2,1)}, bf16[4,384,768]{2,1,0:T(8,128)(2,1)}, f32[4,2,8,128]{3,2,1,0:T(8,128)}) custom-call(s32[2]{0:T(128)} %steps.1, f32[1,128]{1,0:T(1,128)} %constant.8.freqs, bf16[2,1,64,256]{3,2,1,0:T(8,128)(2,1)} %images.1, bf16[2,1,64,256]{3,2,1,0:T(8,128)(2,1)} %out_grad.1, bf16[1,3,3,256,256]{4,3,2,1,0:T(8,128)(2,1)} %weight.1, ...), custom_call_target="tpu_custom_call" | custom-call | tf_op jit(solution)/shard_map/pallas_call | solution.py:443
  45.7 4.2 %shard_map.95 = (f32[1,3,3,256,256]{4,3,2,1,0:T(8,128)}, f32[1,256]{1,0:T(1,128)}, f32[1,256,512]{2,1,0:T(8,128)}) custom-call(bf16[4,256,256]{2,1,0:T(8,128)(2,1)} %get-tuple-element.6.act_in, bf16[4,384,768]{2,1,0:T(8,128)(2,1)} %get-tuple-element.7.cols_in, f32[4,2,8,128]{3,2,1,0:T(8,128)} %get-tuple-element.8.small_in), custom_call_target="tpu_custom_call" | custom-call | tf_op jit(solution)/shard_map/pallas_call | solution.py:485

commit v5 on v4

--- a/solution.py
+++ b/solution.py
@@ -268,10 +268,6 @@
         obuf[...] = (out + convolve(act_cols, plain, 1 - core)).astype(BF16)
         forward_hop.start()
 
-    @pl.when(s == 0)
-    def _():
-        forward_skip.start()
-
     slope[...] = sigmoid * (1.0 + pre * (1.0 - sigmoid))
 
     def share_act():
@@ -284,6 +280,14 @@
     def _():
         share_act()
         turn_weights()
+        forward_hop.wait_send()
+
+    @pl.when(s == 0)
+    def _():
+        forward_skip.start()
+
+    @pl.when(s < last)
+    def _():
         backward_hop.wait_recv()
 
     @pl.when(s == 0)
@@ -318,9 +322,10 @@
 
     @pl.when(s == last)
     def _():
-        backward_skip.start()
         act_sibling.wait_recv()
         share_act()
+        backward_hop.wait_send()
+        backward_skip.start()
 
     small[me, core] = rows_of(sum_normal * gains, sum_pre, sum_normal * scales1, cosines, sines)
     for copy in small_copy:
@@ -367,11 +372,7 @@
             grad_row(k).wait_send()
         backward_skip.wait_send()
 
-    @pl.when(s < last)
-    def _():
-        forward_hop.wait_send()
-
-    @pl.when(s > 0)
+    @pl.when((s > 0) & (s < last))
     def _():
         backward_hop.wait_send()
 

time: 50.8 us -> 50.6 us (level)
  no operation moved by 1% of the time
where the time goes in v5:
time: 50.6 us; the launch traced here: 49.8 us
  Pallas kernels  49.1 us (97%)
  between operations  0.64 us (1%)
    pallas_call x1, Pallas kernels, per_device(): pl.pallas_call(functools.partial(chain_body, n_sec, flips), out_shape=(ja...  44.9 us
    pallas_call x1, Pallas kernels, per_device(): pl.pallas_call(functools.partial(grad_body, 4 if n_dp == 2 else 2), out_s...  4.21 us

profile of v5, /device:TPU:0, one launch (start us, length us, event | category | flops | bytes accessed | tf_op | source)
XLA Modules:
  0.0 49.8 jit_solution(7278662382267127963)
XLA Ops:
  0.6 44.9 %shard_map.94 = (bf16[4,256,256]{2,1,0:T(8,128)(2,1)}, bf16[4,384,768]{2,1,0:T(8,128)(2,1)}, f32[4,2,8,128]{3,2,1,0:T(8,128)}) custom-call(s32[2]{0:T(128)} %steps.1, f32[1,128]{1,0:T(1,128)} %constant.8.freqs, bf16[2,1,64,256]{3,2,1,0:T(8,128)(2,1)} %images.1, bf16[2,1,64,256]{3,2,1,0:T(8,128)(2,1)} %out_grad.1, bf16[1,3,3,256,256]{4,3,2,1,0:T(8,128)(2,1)} %weight.1, ...), custom_call_target="tpu_custom_call" | custom-call | tf_op jit(solution)/shard_map/pallas_call | solution.py:444
  45.6 4.2 %shard_map.95 = (f32[1,3,3,256,256]{4,3,2,1,0:T(8,128)}, f32[1,256]{1,0:T(1,128)}, f32[1,256,512]{2,1,0:T(8,128)}) custom-call(bf16[4,256,256]{2,1,0:T(8,128)(2,1)} %get-tuple-element.6.act_in, bf16[4,384,768]{2,1,0:T(8,128)(2,1)} %get-tuple-element.7.cols_in, f32[4,2,8,128]{3,2,1,0:T(8,128)} %get-tuple-element.8.small_in), custom_call_target="tpu_custom_call" | custom-call | tf_op jit(solution)/shard_map/pallas_call | solution.py:486

commit v6 on v4

v6 whole, which is shorter than its diff:
```python
import functools
import math

import jax
import jax.numpy as jnp
import numpy as np
from jax import lax
from jax.experimental import pallas as pl
from jax.experimental.pallas import tpu as pltpu
from jax.sharding import PartitionSpec as P

G = 32
EPS = 1e-05
MESH = pl.DeviceIdType.MESH
F32 = jnp.float32
BF16 = jnp.bfloat16
PIX = 256
COLS = 64
C = 256


def thirds(x):
    first = x.astype(BF16)
    rest = x - first.astype(F32)
    second = rest.astype(BF16)
    return first, second, (rest - second.astype(F32)).astype(BF16)


def rows_of(*rows):
    index = lax.broadcasted_iota(jnp.int32, (8, rows[0].shape[1]), 0)
    out = jnp.zeros((8, rows[0].shape[1]), F32)
    for i, row in enumerate(rows):
        out = jnp.where(index == i, row, out)
    return out


def group_means(first, second, same, scale):
    parts = [p.astype(F32) for p in thirds(first) + thirds(second)]
    sums = jnp.dot(rows_of(*parts).astype(BF16), same, preferred_element_type=F32) * scale
    return sums[0:1] + (sums[1:2] + sums[2:3]), sums[3:4] + (sums[4:5] + sums[5:6])


def spread_columns(ref, value):
    column = lax.broadcasted_iota(jnp.int32, (PIX, C), 0) & (COLS - 1)
    left = jnp.where(column == 0, 0.0, pltpu.roll(value, 1, 0))
    right = jnp.where(column == COLS - 1, 0.0, pltpu.roll(value, PIX - 1, 0))
    ref[COLS : COLS + PIX, 0:C] = left.astype(BF16)
    ref[COLS : COLS + PIX, C : 2 * C] = value.astype(BF16)
    ref[COLS : COLS + PIX, 2 * C : 3 * C] = right.astype(BF16)


def clear_border(ref):
    blank = jnp.zeros((COLS, 3 * C), BF16)
    ref[0:COLS, :] = blank
    ref[COLS + PIX : 2 * COLS + PIX, :] = blank


def convolve(ref, kernel):
    left = jnp.concatenate([ref[ky * COLS : ky * COLS + PIX, :] for ky in range(3)], axis=1)
    return jnp.dot(left, kernel.reshape(9 * C, C), preferred_element_type=F32)


def chain_body(
    n_sec, flips, steps, freqs, images, out_grad, weight, gain, emb,
    act_out, cols_out, small_out,
    act_t, g_cols, small, hbuf, skip, gskip, obuf, dbuf, g_all, plain, turned, act_cols,
    normed, slope, d_act, steps_v, freqs_v, gain_v, emb_v, send, recv, local, leave,
):
    dp = lax.axis_index("dp")
    s = lax.axis_index("section")
    space = lax.axis_index("space")
    y = space // 2
    last = n_sec - 1
    me = dp * 2 + y if len(flips) == 3 else y
    ahead, behind = lax.rem(s + 1, n_sec), lax.rem(s + n_sec - 1, n_sec)

    def space_peer(k):
        return {"space": space ^ k}

    def plane_peer(k):
        if k == 2:
            return {"space": space ^ 2}
        return {"dp": dp ^ 1, "space": space ^ (k & 2)}

    barrier = pltpu.get_barrier_semaphore()
    partners = [space_peer(k) for k in (1, 2, 3)]
    partners += [plane_peer(k) for k in flips if k != 2]
    partners += [{"section": ahead}, {"section": behind}]
    for partner in partners:
        pl.semaphore_signal(barrier, inc=1, device_id=partner, device_id_type=MESH)

    loads = [
        pltpu.make_async_copy(src, dst, local.at[i])
        for i, (src, dst) in enumerate((
            (steps, steps_v), (freqs, freqs_v), (emb.at[0], emb_v), (gain, gain_v),
            (weight.at[0], plain),
        ))
    ]
    for load in loads:
        load.start()

    def remote(src, dst, number, device):
        return pltpu.make_async_remote_copy(
            src_ref=src, dst_ref=dst, send_sem=send.at[number], recv_sem=recv.at[number],
            device_id=device, device_id_type=MESH,
        )

    def row_at(index):
        return pl.ds(pl.multiple_of(index * COLS, COLS), COLS)

    g_mine = g_all.at[me]
    g_cols_mine = g_cols.at[me]

    def image_row(k):
        return remote(
            images.at[(space ^ k) // 2, 0], hbuf.at[row_at(space), :], k - 1, space_peer(k)
        )

    def grad_row(k):
        return remote(
            out_grad.at[(space ^ k) // 2, 0], g_all.at[me ^ (k >> 1), row_at(space), :],
            k - 1, space_peer(k),
        )

    own_image = pltpu.make_async_copy(images.at[y, 0], hbuf.at[row_at(space), :], local.at[5])
    own_grad = pltpu.make_async_copy(
        out_grad.at[y, 0], g_all.at[me, row_at(space), :], local.at[5]
    )
    forward_hop = remote(obuf, hbuf, 3, {"section": ahead})
    forward_skip = remote(obuf, skip, 4, {"section": behind})
    backward_hop = remote(dbuf, g_mine, 5, {"section": behind})
    backward_skip = remote(dbuf, gskip, 6, {"section": ahead})
    act_copy = {k: remote(act_t.at[me], act_t.at[me], 6 + k, plane_peer(k)) for k in flips}
    g_copy = {k: remote(g_mine, g_mine, 9 + k, plane_peer(k)) for k in flips}
    small_copy = {k: remote(small.at[me], small.at[me], 12 + k, plane_peer(k)) for k in flips}

    for load in loads[:4]:
        load.wait()
    angles = steps_v[y].astype(F32) * freqs_v[...]
    features = jnp.concatenate([jnp.cos(angles), jnp.sin(angles)], axis=1)
    parts = rows_of(*[p.astype(F32) for p in thirds(features)]).astype(BF16)
    embedded = jnp.dot(parts, emb_v[...], preferred_element_type=F32)
    embedded = embedded[0:1] + (embedded[1:2] + embedded[2:3])
    scales1 = 1.0 + embedded[:, :C]
    shifts = embedded[:, C:]
    gains = gain_v[...]
    factor = gains * scales1
    same = (
        lax.broadcasted_iota(jnp.int32, (C, C), 0) // (C // G)
        == lax.broadcasted_iota(jnp.int32, (C, C), 1) // (C // G)
    ).astype(F32).astype(BF16)
    cells = PIX * (C // G)

    clear_border(act_cols)
    for i in range(4):
        clear_border(g_cols.at[i])

    pl.semaphore_wait(barrier, len(partners))

    @pl.when(s == 0)
    def _():
        for k in (1, 2, 3):
            image_row(k).start()

    @pl.when(s == last)
    def _():
        for k in (1, 2, 3):
            grad_row(k).start()

    loads[4].wait()

    def turn_weights():
        for ky in range(3):
            for kx in range(3):
                turned[ky, kx * C : (kx + 1) * C, :] = plain[2 - ky, 2 - kx].T

    def back_convolve():
        spread_columns(g_cols_mine, g_mine[...].astype(F32))
        d_act[...] = convolve(g_cols_mine, turned[...])

    def share_grad():
        for k in flips:
            g_copy[k].start()

    @pl.when(s == 0)
    def _():
        own_image.start()
        own_image.wait()
        for k in (1, 2, 3):
            image_row(k).wait_recv()

    @pl.when(s == last)
    def _():
        own_grad.start()
        turn_weights()
        own_grad.wait()
        for k in (1, 2, 3):
            grad_row(k).wait_recv()
        back_convolve()

    @pl.when(s > 0)
    def _():
        forward_hop.wait_recv()

    @pl.when(s == last)
    def _():
        forward_skip.wait_recv()
        hbuf[...] = (hbuf[...].astype(F32) + skip[...].astype(F32)).astype(BF16)

    tensor = hbuf[...].astype(F32)
    first = jnp.sum(tensor, axis=0, keepdims=True)
    square = jnp.sum(tensor * tensor, axis=0, keepdims=True)
    average, mean_square = group_means(first, square, same, 1.0 / cells)
    inverse = lax.rsqrt(mean_square - average * average + EPS)
    normal = (tensor - average) * inverse
    normed[...] = normal
    pre = normal * factor + shifts
    sigmoid = jax.nn.sigmoid(pre)
    act = pre * sigmoid

    @pl.when(s < last)
    def _():
        spread_columns(act_cols, act)
        out = convolve(act_cols, plain[...])
        obuf[...] = (hbuf[...].astype(F32) + out).astype(BF16)
        forward_hop.start()

    @pl.when(s == 0)
    def _():
        forward_skip.start()

    slope[...] = sigmoid * (1.0 + pre * (1.0 - sigmoid))

    def share_act(value):
        act_t[me] = value.T
        for k in flips:
            act_copy[k].start()

    @pl.when(s < last)
    def _():
        share_act(act.astype(BF16))

    @pl.when(s == last)
    def _():
        obuf[...] = act.astype(BF16)

    @pl.when(s < last)
    def _():
        turn_weights()
        backward_hop.wait_recv()

    @pl.when(s == 0)
    def _():
        backward_skip.wait_recv()
        g_all[me] = (g_mine[...].astype(F32) + gskip[...].astype(F32)).astype(BF16)

    @pl.when(s == 0)
    def _():
        share_grad()

    @pl.when(s < last)
    def _():
        back_convolve()

    d_pre = d_act[...] * slope[...]
    normal = normed[...]
    sum_pre = jnp.sum(d_pre, axis=0, keepdims=True)
    sum_normal = jnp.sum(d_pre * normal, axis=0, keepdims=True)

    @pl.when(s > 0)
    def _():
        mean_d, mean_dn = group_means(sum_pre * factor, sum_normal * factor, same, 1.0 / cells)
        d_tensor = inverse * (d_pre * factor - mean_d - normal * mean_dn)
        dbuf[...] = (g_mine[...].astype(F32) + d_tensor).astype(BF16)
        backward_hop.start()
        share_grad()

    @pl.when(s == last)
    def _():
        backward_skip.start()
        share_act(obuf[...])

    small[me] = rows_of(sum_normal * gains, sum_pre, sum_normal * scales1, features)
    for k in flips:
        small_copy[k].start()

    def image_out(slot, number):
        return [
            pltpu.make_async_copy(act_t.at[slot], act_out.at[slot], leave.at[number]),
            pltpu.make_async_copy(g_cols.at[slot], cols_out.at[slot], leave.at[4 + number]),
        ]

    leaving = image_out(me, 0)
    for copy in leaving:
        copy.start()
    for k in flips:
        act_copy[k].wait_recv()
    for k in flips:
        g_copy[k].wait_recv()
        other = me ^ (((k & 1) << 1) | (k >> 1))
        spread_columns(g_cols.at[other], g_all[other].astype(F32))
        for copy in image_out(other, k):
            copy.start()
            leaving.append(copy)
    for k in flips:
        small_copy[k].wait_recv()
    leaving.append(pltpu.make_async_copy(small, small_out, leave.at[8]))
    leaving[-1].start()

    @pl.when(s == 0)
    def _():
        for k in (1, 2, 3):
            image_row(k).wait_send()
        forward_skip.wait_send()

    @pl.when(s == last)
    def _():
        for k in (1, 2, 3):
            grad_row(k).wait_send()
        backward_skip.wait_send()

    @pl.when(s < last)
    def _():
        forward_hop.wait_send()

    @pl.when(s > 0)
    def _():
        backward_hop.wait_send()

    for k in flips:
        act_copy[k].wait_send()
        g_copy[k].wait_send()
        small_copy[k].wait_send()
    for copy in leaving:
        copy.wait()


def grad_body(
    slots, act_in, cols_in, small_in, conv_out, gain_out, emb_out,
    act_t, g_cols, small, taps, gain_v, emb_v, sems,
):
    loads = [pltpu.make_async_copy(small_in, small, sems.at[11])]
    for i in range(slots):
        loads.append(pltpu.make_async_copy(act_in.at[i], act_t.at[i], sems.at[12 + i]))
        loads.append(pltpu.make_async_copy(cols_in.at[i], g_cols.at[i], sems.at[16 + i]))
    for load in loads:
        load.start()
    loads[0].wait()
    packed = [small[i] for i in range(slots)]
    gain_total = packed[0][2:3]
    for block in packed[1:]:
        gain_total = gain_total + block[2:3]
    gain_v[...] = gain_total
    features = rows_of(*[block[3:4] for block in packed])
    d_rows = rows_of(*[jnp.concatenate([block[0:1], block[1:2]], axis=1) for block in packed])
    emb_v[...] = jnp.dot(
        features.T, d_rows, precision=lax.Precision.HIGHEST, preferred_element_type=F32
    )
    copies = [
        pltpu.make_async_copy(gain_v, gain_out, sems.at[9]),
        pltpu.make_async_copy(emb_v, emb_out.at[0], sems.at[10]),
    ]
    for copy in copies:
        copy.start()
    for load in loads[1:]:
        load.wait()
    left = jnp.concatenate([act_t[i] for i in range(slots)], axis=1)
    for ky in range(3):
        for kx in range(3):
            rows, lanes = slice(ky * COLS, ky * COLS + PIX), slice(kx * C, (kx + 1) * C)
            right = jnp.concatenate([g_cols[i, rows, lanes] for i in range(slots)], axis=0)
            total = jnp.dot(left, right, preferred_element_type=F32)
            tap = ky * 3 + kx
            taps[tap] = total
            copy = pltpu.make_async_copy(taps.at[tap], conv_out.at[0, 2 - ky, 2 - kx], sems.at[tap])
            copy.start()
            copies.append(copy)
    for copy in copies:
        copy.wait()


def per_device(images, steps, out_grad, conv_weight, gn_gain, emb_weight):
    n_dp = lax.axis_size("dp")
    n_sec = lax.axis_size("section")
    flips = (1, 2, 3) if n_dp == 2 else (2,)
    half = C // 2
    freqs = np.exp(-math.log(10000.0) * np.arange(half, dtype=np.float32) / half)
    hbm = pl.BlockSpec(memory_space=pltpu.HBM)
    padded = PIX + 2 * COLS
    chain = pl.pallas_call(
        functools.partial(chain_body, n_sec, flips),
        out_shape=(
            jax.ShapeDtypeStruct((4, C, PIX), BF16),
            jax.ShapeDtypeStruct((4, padded, 3 * C), BF16),
            jax.ShapeDtypeStruct((4, 8, C), F32),
        ),
        in_specs=[hbm] * 7,
        out_specs=(hbm, hbm, hbm),
        scratch_shapes=[
            pltpu.VMEM((4, C, PIX), BF16),
            pltpu.VMEM((4, padded, 3 * C), BF16),
            pltpu.VMEM((4, 8, C), F32),
            pltpu.VMEM((PIX, C), BF16),
            pltpu.VMEM((PIX, C), BF16),
            pltpu.VMEM((PIX, C), BF16),
            pltpu.VMEM((PIX, C), BF16),
            pltpu.VMEM((PIX, C), BF16),
            pltpu.VMEM((4, PIX, C), BF16),
            pltpu.VMEM((3, 3, C, C), BF16),
            pltpu.VMEM((3, 3 * C, C), BF16),
            pltpu.VMEM((padded, 3 * C), BF16),
            pltpu.VMEM((PIX, C), F32),
            pltpu.VMEM((PIX, C), F32),
            pltpu.VMEM((PIX, C), F32),
            pltpu.SMEM((2,), jnp.int32),
            pltpu.VMEM((1, C // 2), F32),
            pltpu.VMEM((1, C), F32),
            pltpu.VMEM((C, 2 * C), BF16),
            pltpu.SemaphoreType.DMA((16,)),
            pltpu.SemaphoreType.DMA((16,)),
            pltpu.SemaphoreType.DMA((6,)),
            pltpu.SemaphoreType.DMA((9,)),
        ],
        compiler_params=pltpu.CompilerParams(
            collective_id=0, has_side_effects=True, vmem_limit_bytes=56 * 1024 * 1024
        ),
    )(
        steps, jnp.asarray(freqs, F32)[None, :], images, out_grad, conv_weight, gn_gain, emb_weight
    )
    grads = pl.pallas_call(
        functools.partial(grad_body, 4 if n_dp == 2 else 2),
        out_shape=(
            jax.ShapeDtypeStruct((1, 3, 3, C, C), F32),
            jax.ShapeDtypeStruct((1, C), F32),
            jax.ShapeDtypeStruct((1, C, 2 * C), F32),
        ),
        in_specs=[hbm] * 3,
        out_specs=(hbm, hbm, hbm),
        scratch_shapes=[
            pltpu.VMEM((4, C, PIX), BF16),
            pltpu.VMEM((4, padded, 3 * C), BF16),
            pltpu.VMEM((4, 8, C), F32),
            pltpu.VMEM((9, C, C), F32),
            pltpu.VMEM((1, C), F32),
            pltpu.VMEM((C, 2 * C), F32),
            pltpu.SemaphoreType.DMA((20,)),
        ],
        compiler_params=pltpu.CompilerParams(vmem_limit_bytes=56 * 1024 * 1024),
    )(*chain)
    if n_dp != 2:
        grads = lax.psum(grads, "dp")
    return grads


def solution(mesh):
    in_specs = (
        P("dp", "space", None, None),
        P("dp"),
        P("dp", "space", None, None),
        P("section", None, None, None, None),
        P("section", None),
        P("section", None, None),
    )
    out_specs = (P("section", None, None, None, None), P("section", None), P("section", None, None))
    return jax.shard_map(
        per_device, mesh=mesh, in_specs=in_specs, out_specs=out_specs, check_vma=False
    )
```

time: 50.8 us -> 52.7 us (1.037); the launches traced: 49.9 us -> 52.5 us
  Pallas kernels: 49.3 us -> 51.9 us
    pallas_call x1, Pallas kernels: 45.1 us -> 47.7 us  [per_device(): pl.pallas_call(functools.partial(chain_body, n_sec, flips), out_shape=(ja...]
where the time goes in v6:
time: 52.7 us; the launch traced here: 52.5 us
  Pallas kernels  51.9 us (98%)
  between operations  0.64 us (1%)
    pallas_call x1, Pallas kernels, per_device(): pl.pallas_call(functools.partial(chain_body, n_sec, flips), out_shape=(ja...  47.7 us
    pallas_call x1, Pallas kernels, per_device(): pl.pallas_call(functools.partial(grad_body, 4 if n_dp == 2 else 2), out_s...  4.21 us

profile of v6, /device:TPU:0, one launch (start us, length us, event | category | flops | bytes accessed | tf_op | source)
XLA Modules:
  0.0 52.5 jit_solution(3608395976246162227)
XLA Ops:
  0.6 47.7 %shard_map.94 = (bf16[4,256,256]{2,1,0:T(8,128)(2,1)}, bf16[4,384,768]{2,1,0:T(8,128)(2,1)}, f32[4,8,256]{2,1,0:T(8,128)}) custom-call(s32[2]{0:T(128)} %steps.1, f32[1,128]{1,0:T(1,128)} %constant.8.freqs, bf16[2,1,64,256]{3,2,1,0:T(8,128)(2,1)} %images.1, bf16[2,1,64,256]{3,2,1,0:T(8,128)(2,1)} %out_grad.1, bf16[1,3,3,256,256]{4,3,2,1,0:T(8,128)(2,1)} %weight.1, ...), custom_call_target="tpu_custom_call" | custom-call | tf_op jit(solution)/shard_map/pallas_call | solution.py:390
  48.3 4.2 %shard_map.95 = (f32[1,3,3,256,256]{4,3,2,1,0:T(8,128)}, f32[1,256]{1,0:T(1,128)}, f32[1,256,512]{2,1,0:T(8,128)}) custom-call(bf16[4,256,256]{2,1,0:T(8,128)(2,1)} %get-tuple-element.6.act_in, bf16[4,384,768]{2,1,0:T(8,128)(2,1)} %get-tuple-element.7.cols_in, f32[4,8,256]{2,1,0:T(8,128)} %get-tuple-element.8.small_in), custom_call_target="tpu_custom_call" | custom-call | tf_op jit(solution)/shard_map/pallas_call | solution.py:430

commit v7 on v5

--- a/solution.py
+++ b/solution.py
@@ -76,7 +76,7 @@
     n_sec, flips, steps, freqs, images, out_grad, weight, gain, emb,
     act_out, cols_out, small_out,
     act_t, g_cols, small, hbuf, skip, gskip, obuf, dbuf, act_raw, g_all, plain, across, turned, act_cols,
-    normed, slope, d_act, steps_v, freqs_v, gain_v, emb_v, send, recv, local, leave,
+    normed, slope, d_act, steps_v, freqs_v, gain_v, emb_v, send, recv, local, leave, ready,
 ):
     dp = lax.axis_index("dp")
     s = lax.axis_index("section")
@@ -94,9 +94,15 @@
     others = [(k, f) for k in (0,) + flips for f in (0, 1) if k or f]
     barrier = pltpu.get_barrier_semaphore()
     partners = [plane_peer(k, f) if k & 1 else {"space": space ^ (k & 2) ^ f} for k, f in others]
-    partners += [{"section": ahead}, {"section": behind}]
     for partner in partners:
         pl.semaphore_signal(barrier, inc=1, device_id=partner, device_id_type=MESH)
+    for partner in (ahead, behind):
+
+        @pl.when(partner != 0)
+        def _():
+            pl.semaphore_signal(
+                barrier, inc=1, device_id={"section": partner}, device_id_type=MESH
+            )
 
     loads = [
         pltpu.make_async_copy(src, dst, local.at[i])
@@ -193,7 +199,17 @@
     ).astype(F32).astype(BF16)
     cells = PIX * (C // G)
 
-    pl.semaphore_wait(barrier, len(partners))
+    @pl.when(s == 0)
+    def _():
+        pl.semaphore_wait(barrier, len(partners))
+
+    @pl.when(s > 0)
+    def _():
+        pl.semaphore_wait(barrier, len(partners) + 2)
+
+    @pl.when((ahead == 0) | (behind == 0))
+    def _():
+        pl.semaphore_signal(ready, inc=1, device_id={"section": 0}, device_id_type=MESH)
 
     @pl.when(s == 0)
     def _():
@@ -266,6 +282,11 @@
         act_sibling.wait_recv()
         spread_columns(act_cols, act_raw[1 - core].astype(F32), 1 - core)
         obuf[...] = (out + convolve(act_cols, plain, 1 - core)).astype(BF16)
+
+        @pl.when(s == 0)
+        def _():
+            pl.semaphore_wait(ready, 2)
+
         forward_hop.start()
 
     slope[...] = sigmoid * (1.0 + pre * (1.0 - sigmoid))
@@ -476,6 +497,7 @@
             pltpu.SemaphoreType.DMA((28,)),
             pltpu.SemaphoreType.DMA((8,)),
             pltpu.SemaphoreType.DMA((9,)),
+            pltpu.SemaphoreType.REGULAR,
         ],
         compiler_params=pltpu.CompilerParams(
             collective_id=0, has_side_effects=True, vmem_limit_bytes=56 * 1024 * 1024

time: 50.6 us -> 48.3 us (0.955)
  Pallas kernels: 49.1 us -> 47.2 us
    pallas_call x1, Pallas kernels: 44.9 us -> 43 us  [per_device(): pl.pallas_call(functools.partial(chain_body, n_sec, flips), out_shape=(ja...]
where the time goes in v7:
time: 48.3 us; the launch traced here: 47.8 us
  Pallas kernels  47.2 us (98%)
  between operations  0.64 us (1%)
    pallas_call x1, Pallas kernels, per_device(): pl.pallas_call(functools.partial(chain_body, n_sec, flips), out_shape=(ja...  43 us
    pallas_call x1, Pallas kernels, per_device(): pl.pallas_call(functools.partial(grad_body, 4 if n_dp == 2 else 2), out_s...  4.21 us

profile of v7, /device:TPU:0, one launch (start us, length us, event | category | flops | bytes accessed | tf_op | source)
XLA Modules:
  0.0 47.8 jit_solution(2663730049143150741)
XLA Ops:
  0.6 43.0 %shard_map.94 = (bf16[4,256,256]{2,1,0:T(8,128)(2,1)}, bf16[4,384,768]{2,1,0:T(8,128)(2,1)}, f32[4,2,8,128]{3,2,1,0:T(8,128)}) custom-call(s32[2]{0:T(128)} %steps.1, f32[1,128]{1,0:T(1,128)} %constant.8.freqs, bf16[2,1,64,256]{3,2,1,0:T(8,128)(2,1)} %images.1, bf16[2,1,64,256]{3,2,1,0:T(8,128)(2,1)} %out_grad.1, bf16[1,3,3,256,256]{4,3,2,1,0:T(8,128)(2,1)} %weight.1, ...), custom_call_target="tpu_custom_call" | custom-call | tf_op jit(solution)/shard_map/pallas_call | solution.py:465
  43.6 4.2 %shard_map.95 = (f32[1,3,3,256,256]{4,3,2,1,0:T(8,128)}, f32[1,256]{1,0:T(1,128)}, f32[1,256,512]{2,1,0:T(8,128)}) custom-call(bf16[4,256,256]{2,1,0:T(8,128)(2,1)} %get-tuple-element.6.act_in, bf16[4,384,768]{2,1,0:T(8,128)(2,1)} %get-tuple-element.7.cols_in, f32[4,2,8,128]{3,2,1,0:T(8,128)} %get-tuple-element.8.small_in), custom_call_target="tpu_custom_call" | custom-call | tf_op jit(solution)/shard_map/pallas_call | solution.py:508

commit v8 on v7

--- a/solution.py
+++ b/solution.py
@@ -297,6 +297,11 @@
             act_copy[k].start()
         act_t[me, half_at(1 - core), :] = act_raw[1 - core].T
 
+    def pass_act():
+        for k in flips:
+            act_copy[k].wait_recv()
+            act_pass[k].start()
+
     @pl.when(s < last)
     def _():
         share_act()
@@ -309,6 +314,7 @@
 
     @pl.when(s < last)
     def _():
+        pass_act()
         backward_hop.wait_recv()
 
     @pl.when(s == 0)
@@ -362,9 +368,10 @@
     for copy in leaving:
         copy.start()
 
-    for k in flips:
-        act_copy[k].wait_recv()
-        act_pass[k].start()
+    @pl.when(s == last)
+    def _():
+        pass_act()
+
     for k in flips:
         g_copy[k].wait_recv()
         g_pass[k].start()

time: 48.3 us -> 48.3 us (level)
  no operation moved by 1% of the time
where the time goes in v8:
time: 48.3 us; the launch traced here: 47.9 us
  Pallas kernels  47.2 us (98%)
  between operations  0.64 us (1%)
    pallas_call x1, Pallas kernels, per_device(): pl.pallas_call(functools.partial(chain_body, n_sec, flips), out_shape=(ja...  43 us
    pallas_call x1, Pallas kernels, per_device(): pl.pallas_call(functools.partial(grad_body, 4 if n_dp == 2 else 2), out_s...  4.21 us

profile of v8, /device:TPU:0, one launch (start us, length us, event | category | flops | bytes accessed | tf_op | source)
XLA Modules:
  0.0 47.9 jit_solution(11275057078258308699)
XLA Ops:
  0.6 43.0 %shard_map.94 = (bf16[4,256,256]{2,1,0:T(8,128)(2,1)}, bf16[4,384,768]{2,1,0:T(8,128)(2,1)}, f32[4,2,8,128]{3,2,1,0:T(8,128)}) custom-call(s32[2]{0:T(128)} %steps.1, f32[1,128]{1,0:T(1,128)} %constant.8.freqs, bf16[2,1,64,256]{3,2,1,0:T(8,128)(2,1)} %images.1, bf16[2,1,64,256]{3,2,1,0:T(8,128)(2,1)} %out_grad.1, bf16[1,3,3,256,256]{4,3,2,1,0:T(8,128)(2,1)} %weight.1, ...), custom_call_target="tpu_custom_call" | custom-call | tf_op jit(solution)/shard_map/pallas_call | solution.py:472
  43.6 4.2 %shard_map.95 = (f32[1,3,3,256,256]{4,3,2,1,0:T(8,128)}, f32[1,256]{1,0:T(1,128)}, f32[1,256,512]{2,1,0:T(8,128)}) custom-call(bf16[4,256,256]{2,1,0:T(8,128)(2,1)} %get-tuple-element.6.act_in, bf16[4,384,768]{2,1,0:T(8,128)(2,1)} %get-tuple-element.7.cols_in, f32[4,2,8,128]{3,2,1,0:T(8,128)} %get-tuple-element.8.small_in), custom_call_target="tpu_custom_call" | custom-call | tf_op jit(solution)/shard_map/pallas_call | solution.py:515
